TPU v7x, 32 devices: a whole 2x2x4 slice. The times are simulated.
32 devices in a mesh: gx: 8 (over y, x, core), gy: 4 (over z).
Axes of the slice: x: 2, y: 2, z: 4, core: 2. Of those that a mesh axis runs over, the one named last changes fastest.
Arguments:
- tokens: bfloat16 [16384, 1024], P(('gx', 'gy')), may hold values from -6 to 6
- expert_ids: int32 [16384, 2], P(('gx', 'gy')), may hold values from 0 to 15, as said below
- gain_attn: bfloat16 [1024], P('gx'), may hold values from 0.099609375 to 1.8984375
- w_qkv: bfloat16 [3, 1024, 1024], P(None, 'gx', 'gy'), may hold values from -0.1875 to 0.1875
- w_out: bfloat16 [1024, 1024], P('gy', 'gx'), may hold values from -1.796875 to 1.796875
- rel_bias: bfloat16 [32, 16], P('gx', 'gy'), may hold values from -4 to 4
- gain_ffn: bfloat16 [1024], P('gx'), may hold values from 0.099609375 to 1.8984375
- router: bfloat16 [1024, 16], P('gx'), may hold values from -0.125 to 0.125
- w_in: bfloat16 [16, 1024, 5632], P('gy', 'gx'), may hold values from -0.1875 to 0.1875
- w_down: bfloat16 [16, 2816, 1024], P('gy', None, 'gx'), may hold values from -0.8984375 to 0.8984375
- cotangent: bfloat16 [16384, 1024], P(('gx', 'gy')), may hold values from -6 to 6
Outputs:
- mixed: bfloat16 [16384, 1024], P(('gx', 'gy'))
- loss: float32 [], replicated
- router_load: float32 [2, 16], replicated
- grad_tokens: float32 [16384, 1024], P(('gx', 'gy'))
- grad_gain_attn: float32 [1024], P('gx')
- grad_w_qkv: float32 [3, 1024, 1024], P(None, 'gx', 'gy')
- grad_w_out: float32 [1024, 1024], P('gy', 'gx')
- grad_rel_bias: float32 [32, 16], P('gx', 'gy')
- grad_gain_ffn: float32 [1024], P('gx')
- grad_router: float32 [1024, 16], P('gx')
- grad_w_in: float32 [16, 1024, 5632], P('gy', 'gx')
- grad_w_down: float32 [16, 2816, 1024], P('gy', None, 'gx')
Inputs may be any that keep to these rules, and one draw needn't show every extreme that they name: `expert_ids`: each row names 2 different experts; every expert is named by some row.
All inputs are finite; a program needn't handle non-finite values.
Results may differ from a plain program's by a relative error of at most 0.029.
Values may be sent and summed in bfloat16 or wider, within the bound.
A program may use at most 320 MiB of HBM per device.

v0:
```python
import functools
import math

import jax
import jax.numpy as jnp
from jax import lax
from jax.experimental import pallas as pl
from jax.experimental.pallas import tpu as pltpu
from jax.sharding import PartitionSpec as P

LEN = 1024
BLK = 256
CAP = 80


bucket_edges = (12, 16, 23, 32, 46, 64, 91)
epsilon = 1e-06
loss_weight = 0.01
masked_score = -1e30


def bucket_of(offset):
    magnitude = jnp.abs(offset)
    far_bucket = 8 + sum(
        ((magnitude >= edge_value).astype(jnp.int32) for edge_value in bucket_edges)
    )
    return jnp.where(magnitude < 8, magnitude, far_bucket) + 16 * (offset > 0).astype(jnp.int32)


def normalize(values):
    row_scale = lax.rsqrt(jnp.mean(values * values, axis=-1, keepdims=True) + epsilon)
    return (values * row_scale, row_scale)


def norm_back(grad_out, normed, row_scale, gain_vector):
    grad_normed = grad_out * gain_vector
    grad_gain = jnp.sum(grad_out * normed, axis=0)
    grad_input = row_scale * (
        grad_normed - normed * jnp.mean(grad_normed * normed, axis=-1, keepdims=True)
    )
    return (grad_input, grad_gain)


def spread_offsets(along_offsets, row_count):
    head_count, span_width = along_offsets.shape
    key_count = span_width - row_count + 1
    tiled_rows = jnp.broadcast_to(
        along_offsets[:, None, :], (head_count, row_count, span_width)
    ).reshape(head_count, row_count * span_width)
    padded = jnp.pad(tiled_rows, ((0, 0), (0, row_count)))
    shaped = padded.reshape(head_count, row_count, span_width + 1)[:, :, :key_count]
    return shaped[:, :, ::-1]


def gather_offsets(score_grid, row_count):
    head_count = score_grid.shape[0]
    key_count = score_grid.shape[2]
    span_width = key_count + row_count - 1
    padded = jnp.pad(score_grid[:, :, ::-1], ((0, 0), (0, 0), (0, row_count)))
    flat_rows = padded.reshape(head_count, row_count * (key_count + row_count))[
        :, : row_count * span_width
    ]
    return jnp.sum(flat_rows.reshape(head_count, row_count, span_width), axis=1)


def offset_table(q_start, row_count, key_count, bucket_count):
    spot_index = jnp.arange(key_count + row_count - 1, dtype=jnp.int32)
    offsets = key_count - 1 - spot_index - q_start
    return (
        bucket_of(offsets)[:, None] == jnp.arange(bucket_count, dtype=jnp.int32)[None, :]
    ).astype(jnp.float32)


def block_scores(query_rows, key_rows, table_float, q_start):
    row_count = query_rows.shape[0]
    depth = query_rows.shape[2]
    key_count = key_rows.shape[0]
    picks_table = offset_table(q_start, row_count, key_count, table_float.shape[0])
    along_offsets = jnp.dot(picks_table, table_float, precision=lax.Precision.HIGHEST).T
    bias_grid = spread_offsets(along_offsets, row_count)
    scores = (
        jnp.einsum("qhd,khd->hqk", query_rows, key_rows, preferred_element_type=jnp.float32)
        / math.sqrt(depth)
        + bias_grid
    )
    query_pos = q_start + jnp.arange(row_count, dtype=jnp.int32)
    key_pos = jnp.arange(key_count, dtype=jnp.int32)
    allowed = key_pos[None, :] // BLK <= query_pos[:, None] // BLK
    return (jnp.where(allowed[None], scores, masked_score), picks_table)


def general_device(
    tokens, expert_ids, gain_attn, w_qkv, w_out, rel_bias, gain_ffn, router, w_in, w_down, cotangent
):
    shard_list = (gain_attn, w_qkv, w_out, rel_bias, gain_ffn, router, w_in, w_down)
    (
        gain_first,
        qkv_weight,
        out_weight,
        bias_table,
        gain_second,
        route_weight,
        inner_weight,
        outer_weight,
    ) = (
        lax.all_gather(shard_list[0], "gx", axis=0, tiled=True),
        lax.all_gather(shard_list[1], "gx", axis=1, tiled=True),
        lax.all_gather(shard_list[2], "gx", axis=1, tiled=True),
        lax.all_gather(shard_list[3], "gx", axis=0, tiled=True),
        lax.all_gather(shard_list[4], "gx", axis=0, tiled=True),
        lax.all_gather(shard_list[5], "gx", axis=0, tiled=True),
        lax.all_gather(shard_list[6], "gx", axis=1, tiled=True),
        lax.all_gather(shard_list[7], "gx", axis=2, tiled=True),
    )
    tok_dev = tokens.shape[0]
    count_x = lax.axis_size("gx")
    count_y = lax.axis_size("gy")
    total_tokens = tok_dev * count_x * count_y
    model_width = tokens.shape[1]
    expert_count = route_weight.shape[1]
    top_count = expert_ids.shape[1]
    local_experts = inner_weight.shape[0]
    head_count = bias_table.shape[1]
    head_width = qkv_weight.shape[2]
    depth = head_width // head_count
    q_rows = min(512, LEN)
    per_seq = LEN // q_rows
    inputs_float = tokens.astype(jnp.float32)
    normed_one, scale_one = normalize(inputs_float)
    first_norm = (normed_one * gain_first.astype(jnp.float32)).astype(jnp.bfloat16)
    group_rows = lax.all_gather(first_norm, "gy", axis=0, tiled=True)
    tok_group = group_rows.shape[0]
    seq_count = tok_group // LEN
    projected = jnp.einsum(
        "td,cdf->tcf", group_rows, qkv_weight, preferred_element_type=jnp.float32
    ).astype(jnp.bfloat16)
    projected = projected.reshape(tok_group, 3, head_count, depth)
    table_float = bias_table.astype(jnp.float32)

    def forward_block(item_index):
        seq_index = item_index // per_seq
        q_start = item_index % per_seq * q_rows
        query_rows = lax.dynamic_slice_in_dim(projected, seq_index * LEN + q_start, q_rows, 0)[:, 0]
        seq_rows = lax.dynamic_slice_in_dim(projected, seq_index * LEN, LEN, 0)
        scores, unused_picks = block_scores(query_rows, seq_rows[:, 1], table_float, q_start)
        row_max = jnp.max(scores, axis=-1, keepdims=True)
        expo_scores = jnp.exp(scores - row_max)
        row_total = jnp.sum(expo_scores, axis=-1, keepdims=True)
        soft_weights = (expo_scores / row_total).astype(jnp.bfloat16)
        block_out = jnp.einsum(
            "hqk,khd->qhd", soft_weights, seq_rows[:, 2], preferred_element_type=jnp.float32
        ).astype(jnp.bfloat16)
        return (block_out.reshape(q_rows, head_width), (row_max + jnp.log(row_total))[:, :, 0])

    attended, log_totals = lax.map(forward_block, jnp.arange(seq_count * per_seq, dtype=jnp.int32))
    attended = attended.reshape(tok_group, head_width)
    attn_sum = lax.psum_scatter(
        jnp.dot(attended, out_weight, preferred_element_type=jnp.float32).astype(jnp.bfloat16),
        "gy",
        scatter_dimension=0,
        tiled=True,
    ).astype(jnp.float32)
    hidden_state = inputs_float + attn_sum
    normed_two, scale_two = normalize(hidden_state)
    second_norm = (normed_two * gain_second.astype(jnp.float32)).astype(jnp.bfloat16)
    logits = jnp.dot(second_norm, route_weight, preferred_element_type=jnp.float32)
    route = jax.nn.softmax(logits, axis=-1)
    chosen = (
        expert_ids.reshape(-1)[:, None] == jnp.arange(expert_count, dtype=jnp.int32)[None, :]
    ).astype(jnp.int32)
    earlier = jnp.cumsum(chosen, axis=0) - chosen
    slot = jnp.sum(earlier * chosen, axis=-1).reshape(tok_dev, top_count)
    kept = (slot < CAP).astype(jnp.float32)
    counts, prob_sums = lax.psum(
        (jnp.sum(chosen, axis=0).astype(jnp.float32), jnp.sum(route, axis=0)), ("gx", "gy")
    )
    loss = expert_count * jnp.sum(counts / (total_tokens * top_count) * (prob_sums / total_tokens))
    router_load = jnp.stack(
        [
            expert_count * counts / (total_tokens * top_count),
            expert_count * prob_sums / total_tokens,
        ],
        axis=0,
    )
    slot_place = expert_ids * CAP + jnp.minimum(slot, CAP - 1)
    buffer_index = jnp.arange(expert_count * CAP, dtype=jnp.int32)[:, None, None]
    hit_table = (buffer_index == slot_place[None]).astype(jnp.float32) * kept[None]
    dispatch_matrix = jnp.sum(hit_table, axis=-1).astype(jnp.bfloat16)
    send_rows = jnp.dot(dispatch_matrix, second_norm, preferred_element_type=jnp.float32).astype(
        jnp.bfloat16
    )
    send_rows = send_rows.reshape(count_y, local_experts, CAP, model_width)
    received = lax.all_to_all(send_rows, "gy", split_axis=0, concat_axis=0, tiled=True)
    upper = jnp.einsum("slcd,ldf->slcf", received, inner_weight, preferred_element_type=jnp.float32)
    half_width = upper.shape[-1] // 2
    hidden_rows = (
        jax.nn.gelu(upper[..., :half_width], approximate=True) * upper[..., half_width:]
    ).astype(jnp.bfloat16)
    expert_out = jnp.einsum(
        "slcf,lfd->slcd", hidden_rows, outer_weight, preferred_element_type=jnp.float32
    ).astype(jnp.bfloat16)
    expert_out, upper, received = (expert_out, upper, received)
    returned = lax.all_to_all(expert_out, "gy", split_axis=0, concat_axis=0, tiled=True).reshape(
        expert_count * CAP, model_width
    )
    picked_rows = jnp.take(returned, slot_place, axis=0).astype(jnp.float32)
    gate_value = jnp.take_along_axis(route, expert_ids, axis=1) * kept
    mixed = hidden_state + jnp.sum(picked_rows * gate_value[:, :, None], axis=1)
    (
        gain_first,
        qkv_weight,
        out_weight,
        bias_table,
        gain_second,
        route_weight,
        inner_weight,
        outer_weight,
    ) = (
        lax.all_gather(shard_list[0], "gx", axis=0, tiled=True),
        lax.all_gather(shard_list[1], "gx", axis=1, tiled=True),
        lax.all_gather(shard_list[2], "gx", axis=1, tiled=True),
        lax.all_gather(shard_list[3], "gx", axis=0, tiled=True),
        lax.all_gather(shard_list[4], "gx", axis=0, tiled=True),
        lax.all_gather(shard_list[5], "gx", axis=0, tiled=True),
        lax.all_gather(shard_list[6], "gx", axis=1, tiled=True),
        lax.all_gather(shard_list[7], "gx", axis=2, tiled=True),
    )
    table_float = bias_table.astype(jnp.float32)
    grad_mixed = cotangent.astype(jnp.float32)
    grad_gate = kept * jnp.sum(grad_mixed[:, None, :] * picked_rows, axis=-1)
    gate_matrix = jnp.sum(hit_table * gate_value[None], axis=-1)
    grad_buffer = jnp.dot(gate_matrix, grad_mixed, precision=lax.Precision.HIGHEST).astype(
        jnp.bfloat16
    )
    grad_expert = lax.all_to_all(
        grad_buffer.reshape(count_y, local_experts, CAP, model_width),
        "gy",
        split_axis=0,
        concat_axis=0,
        tiled=True,
    )
    half_width = upper.shape[-1] // 2
    activated, pull_gelu = jax.vjp(
        lambda gate_part, up_part: jax.nn.gelu(gate_part, approximate=True) * up_part,
        upper[..., :half_width],
        upper[..., half_width:],
    )
    hidden_rows = activated.astype(jnp.bfloat16)
    grad_hidden = jnp.einsum(
        "slcd,lfd->slcf", grad_expert, outer_weight, preferred_element_type=jnp.float32
    )
    grad_outer = jnp.einsum(
        "slcf,slcd->lfd", hidden_rows, grad_expert, preferred_element_type=jnp.float32
    )
    grad_gate_part, grad_up_part = pull_gelu(grad_hidden)
    grad_upper = jnp.concatenate([grad_gate_part, grad_up_part], axis=-1).astype(jnp.bfloat16)
    grad_inner = jnp.einsum(
        "slcd,slcf->ldf", received, grad_upper, preferred_element_type=jnp.float32
    )
    grad_received = jnp.einsum(
        "slcf,ldf->slcd", grad_upper, inner_weight, preferred_element_type=jnp.float32
    ).astype(jnp.bfloat16)
    grad_copies = lax.all_to_all(
        grad_received, "gy", split_axis=0, concat_axis=0, tiled=True
    ).reshape(expert_count * CAP, model_width)
    grad_second = jnp.sum(
        jnp.take(grad_copies, slot_place, axis=0).astype(jnp.float32) * kept[:, :, None], axis=1
    )
    expert_hits = (expert_ids[:, :, None] == jnp.arange(expert_count, dtype=jnp.int32)).astype(
        jnp.float32
    )
    grad_route = (
        jnp.sum(grad_gate[:, :, None] * expert_hits, axis=1)
        + loss_weight * expert_count * (counts / (total_tokens * top_count)) / total_tokens
    )
    grad_logits = (
        route * (grad_route - jnp.sum(route * grad_route, axis=-1, keepdims=True))
    ).astype(jnp.bfloat16)
    grad_router = jnp.dot(second_norm.T, grad_logits, preferred_element_type=jnp.float32)
    grad_second = grad_second + jnp.dot(
        grad_logits, route_weight.T, preferred_element_type=jnp.float32
    )
    grad_hidden_state, grad_gain_second = norm_back(
        grad_second, normed_two, scale_two, gain_second.astype(jnp.float32)
    )
    grad_hidden_state = grad_mixed + grad_hidden_state
    piece_rows = lax.all_gather(grad_hidden_state.astype(jnp.bfloat16), "gy", axis=0, tiled=True)
    grad_out_weight = jnp.einsum(
        "tf,td->fd", attended, piece_rows, preferred_element_type=jnp.float32
    )
    update_rows = jnp.dot(piece_rows, out_weight.T, preferred_element_type=jnp.float32).astype(
        jnp.bfloat16
    )
    grad_out_weight, grad_attended = (grad_out_weight, update_rows)

    def backward_sequence(seq_index):
        seq_rows = lax.dynamic_slice_in_dim(projected, seq_index * LEN, LEN, 0)
        key_rows = seq_rows[:, 1]
        value_rows = seq_rows[:, 2]
        grad_keys = jnp.zeros((LEN, head_count, depth), jnp.float32)
        grad_values = jnp.zeros((LEN, head_count, depth), jnp.float32)
        grad_table = jnp.zeros(table_float.shape, jnp.float32)
        grad_queries = []
        for block_index in range(per_seq):
            q_start = block_index * q_rows
            query_rows = seq_rows[q_start : q_start + q_rows, 0]
            grad_out = lax.dynamic_slice_in_dim(
                grad_attended, seq_index * LEN + q_start, q_rows, 0
            ).reshape(q_rows, head_count, depth)
            scores, picks_table = block_scores(query_rows, key_rows, table_float, q_start)
            block_lse = log_totals[seq_index * per_seq + block_index]
            soft_probs = jnp.exp(scores - block_lse[:, :, None])
            grad_probs = jnp.einsum(
                "qhd,khd->hqk", grad_out, value_rows, preferred_element_type=jnp.float32
            )
            grad_scores = (
                soft_probs * (grad_probs - jnp.sum(soft_probs * grad_probs, axis=-1, keepdims=True))
            ).astype(jnp.bfloat16)
            grad_queries.append(
                jnp.einsum(
                    "hqk,khd->qhd", grad_scores, key_rows, preferred_element_type=jnp.float32
                )
                / math.sqrt(depth)
            )
            grad_keys = grad_keys + jnp.einsum(
                "hqk,qhd->khd", grad_scores, query_rows, preferred_element_type=jnp.float32
            ) / math.sqrt(depth)
            grad_values = grad_values + jnp.einsum(
                "hqk,qhd->khd",
                soft_probs.astype(jnp.bfloat16),
                grad_out,
                preferred_element_type=jnp.float32,
            )
            along_grads = gather_offsets(grad_scores.astype(jnp.float32), q_rows)
            grad_table = grad_table + jnp.dot(
                picks_table.T, along_grads.T, precision=lax.Precision.HIGHEST
            )
        stacked = jnp.stack(
            [jnp.concatenate(grad_queries, axis=0), grad_keys, grad_values], axis=1
        ).astype(jnp.bfloat16)
        return (stacked, grad_table)

    grad_projected, table_parts = lax.map(backward_sequence, jnp.arange(seq_count, dtype=jnp.int32))
    grad_projected = grad_projected.reshape(tok_group, 3, head_width)
    grad_bias_table = jnp.sum(table_parts, axis=0)
    grad_qkv_weight = jnp.einsum(
        "td,tcf->cdf", group_rows, grad_projected, preferred_element_type=jnp.float32
    )
    grad_slice = lax.slice_in_dim(grad_projected, 0, tok_dev * lax.axis_size("gy"), axis=0)
    grad_first = lax.psum_scatter(
        jnp.einsum(
            "tcf,cdf->td", grad_slice, qkv_weight, preferred_element_type=jnp.float32
        ).astype(jnp.bfloat16),
        "gy",
        scatter_dimension=0,
        tiled=True,
    ).astype(jnp.float32)
    grad_inputs, grad_gain_first = norm_back(
        grad_first, normed_one, scale_one, gain_first.astype(jnp.float32)
    )
    grad_tokens = grad_hidden_state + grad_inputs
    grad_gain_first, grad_gain_second, grad_router = (
        lax.psum(grad_gain_first.astype(jnp.bfloat16), "gy").astype(jnp.float32),
        lax.psum(grad_gain_second.astype(jnp.bfloat16), "gy").astype(jnp.float32),
        lax.psum(grad_router.astype(jnp.bfloat16), "gy").astype(jnp.float32),
    )
    summed_grads = (
        lax.psum_scatter(
            grad_gain_first.astype(jnp.bfloat16), "gx", scatter_dimension=0, tiled=True
        ).astype(jnp.float32),
        lax.psum_scatter(
            grad_qkv_weight.astype(jnp.bfloat16), "gx", scatter_dimension=1, tiled=True
        ).astype(jnp.float32),
        lax.psum_scatter(
            grad_out_weight.astype(jnp.bfloat16), "gx", scatter_dimension=1, tiled=True
        ).astype(jnp.float32),
        lax.psum_scatter(
            grad_bias_table.astype(jnp.bfloat16), "gx", scatter_dimension=0, tiled=True
        ).astype(jnp.float32),
        lax.psum_scatter(
            grad_gain_second.astype(jnp.bfloat16), "gx", scatter_dimension=0, tiled=True
        ).astype(jnp.float32),
        lax.psum_scatter(
            grad_router.astype(jnp.bfloat16), "gx", scatter_dimension=0, tiled=True
        ).astype(jnp.float32),
        lax.psum_scatter(
            grad_inner.astype(jnp.bfloat16), "gx", scatter_dimension=1, tiled=True
        ).astype(jnp.float32),
        lax.psum_scatter(
            grad_outer.astype(jnp.bfloat16), "gx", scatter_dimension=2, tiled=True
        ).astype(jnp.float32),
    )
    return (
        mixed.astype(jnp.bfloat16),
        loss,
        router_load,
        grad_tokens,
        summed_grads[0],
        summed_grads[1],
        summed_grads[2],
        summed_grads[3],
        summed_grads[4],
        summed_grads[5],
        summed_grads[6],
        summed_grads[7],
    )


def dot_nn(a, b):
    return lax.dot_general(a, b, (((1,), (0,)), ((), ())), preferred_element_type=jnp.float32)

def dot_nt(a, b):
    return lax.dot_general(a, b, (((1,), (1,)), ((), ())), preferred_element_type=jnp.float32)

def span_buckets():
    k = jnp.arange(2 * BLK, dtype=jnp.int32)
    return jnp.stack([bucket_of(BLK - k - BLK * d) for d in range(2)])

AXES = ("gx", "gy")
MESH_ID = pl.DeviceIdType.MESH


def fits_fast(mesh):
    return mesh.shape["gx"] == 8 and mesh.shape["gy"] == 4


def places():
    x = lax.axis_index("gx")
    z = lax.axis_index("gy")
    core = x % 2
    chip = x // 2
    along_z = (z + 1 - 2 * (z % 2), (z + 2) % 4, 3 - z)
    chips = (chip + 1 - 2 * (chip % 2), (chip + 2) % 4, 3 - chip)
    return x, z, along_z, tuple(2 * other + core for other in chips), x + 1 - 2 * core


def attend_front(pair, proj_ref, span_ref, tile_ref, attended_ref, lse_ref, kept_ref):
    length = proj_ref.shape[1]
    blocks = length // BLK
    depth = 64
    wide = 2 * depth
    here = slice(pair * wide, (pair + 1) * wide)
    lane = lax.broadcasted_iota(jnp.int32, (1, wide), 1)
    for h in range(2):
        for d in range(2):
            row = span_ref[d, 2 * pair + h:2 * pair + h + 1, :]
            spread = jnp.broadcast_to(row, (BLK, 2 * BLK))
            turned = pltpu.roll(spread, 0, 1, stride=1, stride_axis=0)
            tile_ref[h, d] = turned[:, BLK:]
            kept_ref[2 * pair + h, d] = turned[:, BLK:].astype(jnp.bfloat16)
    far = [span_ref[1, 2 * pair + h:2 * pair + h + 1, 2 * BLK - 1:2 * BLK] for h in range(2)]
    keys = proj_ref[1, :, here]
    values_t = proj_ref[2, :, here].T
    for block in range(blocks):
        rows = pl.ds(block * BLK, BLK)
        query = proj_ref[0, rows, here] * jnp.bfloat16(0.125)
        key_count = (block + 1) * BLK
        outs = []
        for h in range(2):
            picked = jnp.where((lane // depth) == h, query, jnp.bfloat16(0))
            scores = dot_nt(keys[:key_count], picked)
            parts = []
            for kb in range(block + 1):
                part = scores[kb * BLK:(kb + 1) * BLK]
                d = block - kb
                parts.append(part + (tile_ref[h, d] if d < 2 else far[h]))
            top = functools.reduce(jnp.maximum, [jnp.max(p, axis=0, keepdims=True) for p in parts])
            parts = [jnp.exp(p - top) for p in parts]
            total = functools.reduce(jnp.add, [jnp.sum(p, axis=0, keepdims=True) for p in parts])
            scale = 1.0 / total
            weights = jnp.concatenate([(p * scale).astype(jnp.bfloat16) for p in parts], axis=0)
            outs.append(dot_nn(values_t[h * depth:(h + 1) * depth, :key_count], weights))
            lse_ref[pair, h:h + 1, rows] = top + jnp.log(total)
        attended_ref[rows, here] = jnp.concatenate(outs, axis=0).T.astype(jnp.bfloat16)


def front_kernel(
    tok_ref, wq_ref, wo_ref, small_ref, inner_ref, grads_ref, picks_ref,
    seq_out, wqs_out, wos_out, smalls_out, proj_ref, att_ref, lse_ref, kept_ref, inner_a_ref, inner_b_ref, far_ref,
    seq_ref, wqs_ref, wos_ref, smalls_ref, normed_ref, attended_ref, got_ref, span_ref, tile_ref,
    send_sem, recv_sem, local_sem, out_sem,
):
    x, z, along_z, across, sibling = places()
    half = z % 2
    f32, bf16 = jnp.float32, jnp.bfloat16
    peers = [(x, other) for other in along_z] + [(other, z) for other in across] + [(sibling, z)]
    far_peers = [(device, plane) for plane in along_z[1:] for device in (x,) + across]
    peers += [peer for n, peer in enumerate(far_peers) if n % 4]
    barrier = pltpu.get_barrier_semaphore()
    for peer in peers:
        pl.semaphore_signal(barrier, inc=1, device_id=peer, device_id_type=MESH_ID)
    depth = wq_ref.shape[1]
    group = wq_ref.shape[2]
    rows_out = wo_ref.shape[0]
    rows, width = tok_ref.shape

    def qkv_part(owner, slot):
        return wqs_ref.at[:, pl.ds(pl.multiple_of(owner * depth, depth), depth), pl.ds(slot * group, group)]

    def out_part(owner, slot, slots):
        return wos_ref.at[
            pl.ds(slot * rows_out, slots * rows_out), pl.ds(pl.multiple_of(owner * depth, depth), depth)
        ]

    keeps = [
        pltpu.make_async_copy(source, target, local_sem.at[n])
        for n, (source, target) in enumerate(
            ((small_ref, smalls_ref.at[0, x]), (wo_ref, out_part(x, 0, 1)), (wq_ref, qkv_part(x, 0)),
             (tok_ref, seq_ref.at[half]))
        )
    ]
    for copy in keeps:
        copy.start()
    pl.semaphore_wait(barrier, len(peers))
    started = []

    def send(source, target, device):
        index = len(started)
        copy = pltpu.make_async_remote_copy(
            src_ref=source, dst_ref=target, send_sem=send_sem.at[index], recv_sem=recv_sem.at[index],
            device_id=device, device_id_type=MESH_ID,
        )
        copy.start()
        started.append(copy)
        return copy

    out_slots = (2, 1, 3)
    near = across + (sibling,)
    small_z = [send(small_ref, smalls_ref.at[j + 1, x], (x, along_z[j])) for j in range(3)]
    wq_z = send(wq_ref, qkv_part(x, 1), (x, along_z[1]))
    wq_first = [send(wq_ref, qkv_part(x, 0), (other, z)) for other in near]
    tok_z = send(tok_ref, seq_ref.at[half], (x, along_z[0]))
    wo_z = [send(wo_ref, out_part(x, out_slots[j], 1), (x, along_z[j])) for j in range(3)]
    keeps[0].wait()
    for copy in small_z:
        copy.wait_recv()
    small_x = [send(smalls_ref.at[:, x], smalls_ref.at[:, x], (other, z)) for other in near]
    wq_z.wait_recv()
    wq_second = [send(qkv_part(x, 1), qkv_part(x, 1), (other, z)) for other in near]
    far_copies = [
        send(grads_ref.at[(device // 2) * 4 + plane], far_ref.at[n // 4, x // 2], (device, plane))
        for n, (device, plane) in enumerate(far_peers)
    ]
    small_on = []
    first_on = []
    for j in range(3):
        owner = across[j]
        small_x[j].wait_recv()
        small_on.append(send(smalls_ref.at[:, owner], smalls_ref.at[:, owner], (sibling, z)))
        wq_first[j].wait_recv()
        first_on.append(send(qkv_part(owner, 0), qkv_part(owner, 0), (sibling, z)))
    for copy in [small_x[3], wq_first[3]] + small_on + first_on:
        copy.wait_recv()
    for copy in keeps[1:]:
        copy.wait()
    inner_copies = [
        send(inner_ref.at[device // 2], target, (device, z))
        for device, target in zip(across[:2], (inner_a_ref, inner_b_ref))
    ]

    own_smalls = [smalls_ref[0, g].astype(f32) for g in range(8)]
    gain = jnp.concatenate([part[16:17, :] for part in own_smalls], axis=1)
    heads = span_ref.shape[1] // 2
    lanes = lax.broadcasted_iota(jnp.int32, (1, depth), 1)
    table = jnp.concatenate([part[18:22, :] for part in own_smalls], axis=0)
    other_table = jnp.concatenate([smalls_ref[2, g].astype(f32)[18:22, :] for g in range(8)], axis=0)
    table = jnp.where(lanes < heads, table, pltpu.roll(other_table, heads, 1))
    table = jnp.where(lanes < 2 * heads, table, 0.0)
    table = jnp.concatenate([table, jnp.zeros((depth - table.shape[0], depth), f32)], axis=0)
    table = table.T[:2 * heads, :].astype(bf16)
    for d in range(2):
        span_ref[d] = dot_nt(table, picks_ref[d])
    step = rows // 2

    def norm(side, i):
        normed, _ = normalize(seq_ref[side, i * step:(i + 1) * step, :].astype(f32))
        here = pl.ds(pl.multiple_of(side * rows + i * step, step), step)
        normed_ref[here, :] = (normed * gain).astype(bf16)

    for i in range(2):
        norm(half, i)
    tok_z.wait_recv()
    for i in range(2):
        norm(1 - half, i)

    def project(slot):
        here = slice(slot * group, (slot + 1) * group)
        for c in range(3):
            proj_ref[c, :, here] = dot_nn(normed_ref[...], wqs_ref[c, :, here]).astype(bf16)

    def attend(pair):
        attend_front(pair, proj_ref, span_ref, tile_ref, attended_ref, lse_ref, kept_ref)

    def exchange(slot):
        here = pl.ds(slot * group, group)
        there = pl.ds(pl.multiple_of((1 - half) * rows, rows), rows)
        return send(attended_ref.at[there, here], got_ref.at[:, here], (x, along_z[0]))

    project(0)
    for copy in wo_z:
        copy.wait_recv()
    wo_x = [send(out_part(x, 0, 4), out_part(x, 0, 4), (other, z)) for other in near]
    second_on = []
    for j in range(3):
        owner = across[j]
        wq_second[j].wait_recv()
        second_on.append(send(qkv_part(owner, 1), qkv_part(owner, 1), (sibling, z)))
    attend(0)
    wo_on = []
    for j in range(3):
        owner = across[j]
        wo_x[j].wait_recv()
        wo_on.append(send(out_part(owner, 0, 4), out_part(owner, 0, 4), (sibling, z)))
    attend(1)
    got_0 = exchange(0)
    for copy in [wq_second[3]] + second_on:
        copy.wait_recv()
    project(1)
    outs = [
        pltpu.make_async_copy(source, target, out_sem.at[n])
        for n, (source, target) in enumerate(((seq_ref, seq_out), (smalls_ref, smalls_out), (wqs_ref, wqs_out)))
    ]
    for copy in outs:
        copy.start()
    attend(2)
    attend(3)
    got_1 = exchange(1)
    for copy in [wo_x[3]] + wo_on:
        copy.wait_recv()
    outs.append(pltpu.make_async_copy(wos_ref, wos_out, out_sem.at[3]))
    outs[3].start()
    own = pl.ds(pl.multiple_of(half * rows, rows), rows)
    att_ref[:, :2 * group] = attended_ref[own, :]
    for copy in (got_0, got_1):
        copy.wait_recv()
    att_ref[:, 2 * group:] = got_ref[...]
    for copy in inner_copies + far_copies:
        copy.wait_recv()
    for copy in started:
        copy.wait_send()
    for copy in outs:
        copy.wait()


def run_front(tokens, w_qkv, w_out, small, w_in, grad_rows, picks):
    rows, width = tokens.shape
    group = w_qkv.shape[2]
    f32, bf16 = jnp.float32, jnp.bfloat16
    heads = 2 * group // 64
    anywhere = pl.BlockSpec(memory_space=pl.ANY)
    inside = pl.BlockSpec(memory_space=pltpu.VMEM)
    seq = (2, rows, width)
    wqs = (3, width, 2 * group)
    wos = (width, width)
    smalls = (4, 8) + small.shape
    copies_count = 3 + 1 + 4 + 1 + 3 + 4 + 4 + 3 + 3 + 4 + 3 + 3 + 2 + 2 + 8
    return pl.pallas_call(
        front_kernel,
        out_shape=(
            jax.ShapeDtypeStruct(seq, bf16),
            jax.ShapeDtypeStruct(wqs, bf16),
            jax.ShapeDtypeStruct(wos, bf16),
            jax.ShapeDtypeStruct(smalls, bf16),
            jax.ShapeDtypeStruct((3, 2 * rows, 2 * group), bf16),
            jax.ShapeDtypeStruct((rows, width), bf16),
            jax.ShapeDtypeStruct((heads // 2, 2, 2 * rows), f32),
            jax.ShapeDtypeStruct((heads, 2, BLK, BLK), bf16),
            jax.ShapeDtypeStruct(w_in.shape[1:], bf16),
            jax.ShapeDtypeStruct(w_in.shape[1:], bf16),
            jax.ShapeDtypeStruct((2, 4) + grad_rows.shape[1:], bf16),
        ),
        in_specs=[anywhere] * 6 + [inside],
        out_specs=(anywhere,) * 4 + (inside,) * 4 + (anywhere,) * 3,
        scratch_shapes=[
            pltpu.VMEM(seq, bf16),
            pltpu.VMEM(wqs, bf16),
            pltpu.VMEM(wos, bf16),
            pltpu.VMEM(smalls, bf16),
            pltpu.VMEM((2 * rows, width), bf16),
            pltpu.VMEM((2 * rows, 2 * group), bf16),
            pltpu.VMEM((rows, 2 * group), bf16),
            pltpu.VMEM((2, heads, 2 * BLK), f32),
            pltpu.VMEM((2, 2, BLK, BLK), f32),
            pltpu.SemaphoreType.DMA((copies_count,)),
            pltpu.SemaphoreType.DMA((copies_count,)),
            pltpu.SemaphoreType.DMA((4,)),
            pltpu.SemaphoreType.DMA((4,)),
        ],
        compiler_params=pltpu.CompilerParams(
            collective_id=0, has_side_effects=True, vmem_limit_bytes=56 * 2**20
        ),
        cost_estimate=pl.CostEstimate(flops=60 * 10**9, bytes_accessed=30 * 2**20, transcendentals=0),
        name="run_front",
    )(tokens, w_qkv, w_out, small, w_in, grad_rows, picks)


def swap_z(values, step):
    return lax.ppermute(values, "gy", [(i, i ^ step) for i in range(4)])


def exchange_chips(blocks):
    groups = [[2 * c + h for c in range(4)] for h in range(2)]
    return lax.all_to_all(blocks, "gx", 0, 0, axis_index_groups=groups, tiled=True)


def expert_kernel(
    rows_ref, gates_ref, grads_ref, far_ref, inner_ref, inner_a_ref, inner_b_ref, outer_ref,
    returned_ref, copies_ref, ginner_ref, gouter_ref, inner_in_ref,
    x_ref, x_t_ref, dy_ref, gates_in_ref, win_ref, wout_ref, upper_ref, hid_ref, out_ref, back_ref,
    stage_in_ref, stage_out_ref, add_in_ref, outer_in_ref,
    row_send, row_recv, gate_send, gate_recv, out_send, out_recv, copy_send, copy_recv,
    grad_send, grad_recv, w_send, w_recv, part_send, part_recv, gout_send, gout_recv, local_sem, join_sem,
):
    x, z, along_z, across, sibling = places()
    core = x % 2
    chip = x // 2
    me = chip * 4 + z
    _, _, slots, width = x_ref.shape
    chunk = 4 * slots
    tokens = 4 * chunk
    hidden = hid_ref.shape[1]
    half = stage_out_ref.shape[2]
    tiles = hidden // half
    shard = width // 8
    f32, bf16 = jnp.float32, jnp.bfloat16
    planes = (z,) + along_z
    chips = (chip,) + tuple(device // 2 for device in across)
    pair = (sibling, z)

    peers = [(m, k) for m in range(4) for k in range(4) if m or k]
    barrier = pltpu.get_barrier_semaphore()
    for m, k in peers:
        pl.semaphore_signal(
            barrier, inc=1, device_id=(2 * chips[k] + core, planes[m]), device_id_type=MESH_ID
        )
    pl.semaphore_signal(barrier, inc=1, device_id=pair, device_id_type=MESH_ID)
    pl.semaphore_wait(barrier, len(peers) + 1)

    def remote(source, target, sems, index, device):
        return pltpu.make_async_remote_copy(
            src_ref=source, dst_ref=target, send_sem=sems[0].at[index], recv_sem=sems[1].at[index],
            device_id=device, device_id_type=MESH_ID,
        )

    def to_plane(m, source_of, target_of, sems):
        return [
            remote(
                source_of(m, chips[k]), target_of(m), sems, 4 * m + k, (2 * chips[k] + core, planes[m])
            )
            for k in range(4)
            if m or k
        ]

    def lanes_of(owner):
        return pl.ds(pl.multiple_of(owner * shard, shard), shard)

    row_copies = [
        to_plane(
            m, lambda m, c: rows_ref.at[c * 4 + planes[m]], lambda m: x_ref.at[m, chip], (row_send, row_recv)
        )
        for m in range(4)
    ]
    gate_copies = [
        to_plane(
            m, lambda m, c: gates_ref.at[c * 4 + planes[m]], lambda m: gates_in_ref.at[m, chip],
            (gate_send, gate_recv),
        )
        for m in range(4)
    ]
    keeps = [
        pltpu.make_async_copy(inner_ref.at[chip], win_ref.at[chip, core], local_sem.at[0]),
        pltpu.make_async_copy(inner_a_ref, win_ref.at[chips[1], core], local_sem.at[1]),
        pltpu.make_async_copy(inner_b_ref, win_ref.at[chips[2], core], local_sem.at[2]),
        pltpu.make_async_copy(grads_ref.at[me], dy_ref.at[0, chip], local_sem.at[3]),
        pltpu.make_async_copy(rows_ref.at[me], x_ref.at[0, chip], local_sem.at[4]),
        pltpu.make_async_copy(gates_ref.at[me], gates_in_ref.at[0, chip], local_sem.at[5]),
        pltpu.make_async_copy(outer_ref.at[chip], wout_ref.at[:, lanes_of(x)], local_sem.at[6]),
    ]
    pair_inner = [
        remote(source, win_ref.at[chips[k], core], (w_send, w_recv), k, pair)
        for k, source in enumerate((inner_ref.at[chip], inner_a_ref, inner_b_ref))
    ]
    far_inner = remote(inner_ref.at[chips[3]], win_ref.at[chip, core], (w_send, w_recv), 3, (across[2], z))
    far_block = win_ref.at[chips[3], core]
    pair_far = remote(far_block, far_block, (w_send, w_recv), 11, pair)
    outer_copies = [
        remote(outer_ref.at[device // 2], wout_ref.at[:, lanes_of(x)], (w_send, w_recv), 4 + j, (device, z))
        for j, device in enumerate(across)
    ]
    pair_outer = [remote(outer_ref.at[chip], wout_ref.at[:, lanes_of(x)], (w_send, w_recv), 7, pair)] + [
        remote(wout_ref.at[:, lanes_of(device)], wout_ref.at[:, lanes_of(device)], (w_send, w_recv), 8 + j, pair)
        for j, device in enumerate(across)
    ]
    for m in ROW_ORDER:
        for copy in row_copies[m]:
            copy.start()
    far_inner.start()
    for copy in keeps + pair_inner + outer_copies + pair_outer[:1]:
        copy.start()
    for m in range(4):
        for copy in gate_copies[m]:
            copy.start()
    grad_copies = [
        to_plane(
            m, lambda m, c: grads_ref.at[c * 4 + planes[m]], lambda m: dy_ref.at[m, chip], (grad_send, grad_recv)
        )
        for m in range(2)
    ]
    far_grads = pltpu.make_async_copy(far_ref, dy_ref.at[pl.ds(2, 2)], local_sem.at[9])
    far_grads.start()
    for copy in keeps:
        copy.wait()
    for copy in pair_inner:
        copy.wait()
    far_inner.wait_recv()
    pair_far.start()
    pair_far.wait()

    def cols(tile, part):
        return pl.ds(pl.multiple_of(part * hidden + tile * half, half), half)

    def weight(tile, part):
        return win_ref[:, :, :, cols(tile, part)].reshape(width, half)

    def block(m):
        return pl.ds(m * chunk, chunk)

    def widen(m):
        for copy in row_copies[m]:
            copy.wait_recv()
        rows = x_ref.at[m]

        def step(tile, carry):
            values = rows[...].reshape(chunk, width)
            gate = dot_nn(values, weight(tile, 0))
            up = dot_nn(values, weight(tile, 1))
            square = gate * gate
            bent = jnp.tanh(gate * (0.7978845608028654 + 0.03567740813636141 * square))
            lifted = 0.5 + 0.5 * bent
            slope = lifted + (0.5 * gate) * (1.0 - bent * bent) * (
                0.7978845608028654 + 0.10703222440908423 * square
            )
            active = gate * lifted
            upper_ref[block(m), cols(tile, 0)] = (up * slope).astype(bf16)
            upper_ref[block(m), cols(tile, 1)] = active.astype(bf16)
            hid_ref[block(m), cols(tile, 0)] = (active * up).astype(bf16)
            return carry

        lax.fori_loop(0, tiles, step, 0)

    def narrow(m):
        def step(part, carry):
            here = pl.ds(pl.multiple_of(part * 256, 256), 256)
            values = dot_nn(hid_ref[block(m), :], wout_ref[:, here])
            out_ref[m, :, :, here] = values.astype(bf16).reshape(4, slots, 256)
            return carry

        lax.fori_loop(0, width // 256, step, 0)

    out_copies = [
        to_plane(m, lambda m, c: out_ref.at[m, c], lambda m: returned_ref.at[me], (out_send, out_recv))
        for m in range(4)
    ]
    own_out = pltpu.make_async_copy(out_ref.at[0, chip], returned_ref.at[me], local_sem.at[7])
    widen(0)
    widen(1)
    for m in range(4):
        for copy in row_copies[m]:
            copy.wait_send()
    for m in range(2):
        for copy in grad_copies[m]:
            copy.start()
    for j, copy in enumerate(outer_copies):
        copy.wait_recv()
        pair_outer[1 + j].start()
    for copy in outer_copies:
        copy.wait_send()
    for copy in pair_outer:
        copy.wait()
    for m in range(4):
        if m >= 2:
            widen(m)
        narrow(m)
        for copy in out_copies[m]:
            copy.start()
    own_out.start()
    x_t_ref[...] = x_ref[...].reshape(tokens, width).T.reshape(x_t_ref.shape)

    far_grads.wait()
    for m in range(4):
        for copy in gate_copies[m] + (grad_copies[m] if m < 2 else []):
            copy.wait_recv()
        for j in range(4):
            gates = gates_in_ref[m, j].T[:slots, 0:1]
            dy_ref[m, j] = (dy_ref[m, j].astype(f32) * gates).astype(bf16)

    def outer_part(tile):
        slot = lax.rem(tile, STAGES)
        return remote(stage_out_ref.at[slot], outer_in_ref.at[tile], (part_send, part_recv), tiles + tile, pair)

    def weigh_outer(tile, carry):
        slot = lax.rem(tile, STAGES)

        @pl.when(tile >= STAGES)
        def _():
            outer_part(tile - STAGES).wait_send()

        grad_down = dot_nn(hid_ref[:, cols(tile, 0)].T, dy_ref[...].reshape(tokens, width))
        for j in range(4):
            low = grad_down[:, (2 * j) * shard:(2 * j + 1) * shard].astype(bf16)
            high = grad_down[:, (2 * j + 1) * shard:(2 * j + 2) * shard].astype(bf16)
            stage_out_ref[slot, j] = jnp.where(core == 0, high, low)
            hid_ref[pl.ds((j // 2) * half, half), pl.ds(pl.multiple_of(tile * half + (j % 2) * shard, shard), shard)] = (
                jnp.where(core == 0, low, high)
            )
        outer_part(tile).start()
        return carry

    lax.fori_loop(0, tiles, weigh_outer, 0)
    for tile in range(tiles - STAGES, tiles):
        outer_part(tile).wait_send()

    def join_outer(tile, carry):
        outer_part(tile).wait_recv()
        for j in range(4):
            own = hid_ref[pl.ds((j // 2) * half, half), pl.ds(pl.multiple_of(tile * half + (j % 2) * shard, shard), shard)]
            outer_in_ref[tile, j] = (own.astype(f32) + outer_in_ref[tile, j].astype(f32)).astype(bf16)
        return carry

    lax.fori_loop(0, tiles, join_outer, 0)
    own_gout = pltpu.make_async_copy(outer_in_ref.at[:, chip], gouter_ref.at[chip], local_sem.at[3])
    own_gout.start()
    gout_copies = [
        remote(outer_in_ref.at[:, device // 2], gouter_ref.at[chip], (gout_send, gout_recv), j, (device, z))
        for j, device in enumerate(across)
    ]
    for copy in gout_copies:
        copy.start()

    def back(first, count):
        here_rows = pl.ds(first * chunk, count * chunk)

        def step(tile, carry):
            down = wout_ref[pl.ds(pl.multiple_of(tile * half, half), half), :]
            grads = dy_ref[first:first + count].reshape(count * chunk, width)
            grad_hidden = dot_nt(grads, down)
            for part in range(2):
                slope = upper_ref[here_rows, cols(tile, part)].astype(f32)
                upper_ref[here_rows, cols(tile, part)] = (grad_hidden * slope).astype(bf16)
            return carry

        lax.fori_loop(0, tiles, step, 0)

        def gather(j, carry):
            here = pl.ds(pl.multiple_of(j * 256, 256), 256)
            weights = win_ref[j].reshape(2 * shard, 2 * hidden)
            values = dot_nt(upper_ref[here_rows, :], weights)
            back_ref[first:first + count, :, :, here] = values.astype(bf16).reshape(count, 4, slots, 256)
            return carry

        lax.fori_loop(0, 4, gather, 0)

    copy_copies = [
        to_plane(m, lambda m, c: back_ref.at[m, c], lambda m: copies_ref.at[me], (copy_send, copy_recv))
        for m in range(4)
    ]
    own_copy = pltpu.make_async_copy(back_ref.at[0, chip], copies_ref.at[me], local_sem.at[8])
    for first in range(0, 4, BACK_COUNT):
        back(first, BACK_COUNT)
        for m in range(first, first + BACK_COUNT):
            for copy in copy_copies[m]:
                copy.start()
    own_copy.start()

    def inner_part(tile):
        slot = lax.rem(tile, STAGES)
        return remote(stage_in_ref.at[slot], inner_in_ref.at[tile], (part_send, part_recv), tile, pair)

    def inner_load(tile):
        slot = lax.rem(tile, 2)
        return pltpu.make_async_copy(inner_in_ref.at[tile], add_in_ref.at[slot], join_sem.at[slot])

    def inner_stores(tile):
        slot = lax.rem(tile, 2)
        return [
            pltpu.make_async_copy(
                add_in_ref.at[slot, part], ginner_ref.at[:, :, cols(tile, part)], join_sem.at[2 + 2 * slot + part]
            )
            for part in range(2)
        ]

    def join_begin(tile):
        inner_part(tile).wait_recv()

        @pl.when(tile >= 2)
        def _():
            for copy in inner_stores(tile - 2):
                copy.wait()

        inner_load(tile).start()

    def join_end(tile):
        slot = lax.rem(tile, 2)
        inner_load(tile).wait()
        for part in range(2):
            own = upper_ref[pl.ds(0, width // 2), cols(tile, part)].astype(f32)
            other = add_in_ref[slot, part].reshape(width // 2, half).astype(f32)
            add_in_ref[slot, part] = (own + other).astype(bf16).reshape(4, shard, half)
        for copy in inner_stores(tile):
            copy.start()

    def weigh_inner(tile, carry):
        slot = lax.rem(tile, STAGES)

        @pl.when(tile >= LAG)
        def _():
            join_begin(tile - LAG)

        @pl.when(tile >= STAGES)
        def _():
            inner_part(tile - STAGES).wait_send()

        for part in range(2):
            grad_upper = upper_ref[:, cols(tile, part)]
            other = x_t_ref[:, 1 - core].reshape(width // 2, tokens)
            stage_in_ref[slot, part] = dot_nn(other, grad_upper).astype(bf16).reshape(4, shard, half)
        inner_part(tile).start()
        for part in range(2):
            grad_upper = upper_ref[:, cols(tile, part)]
            own = x_t_ref[:, core].reshape(width // 2, tokens)
            upper_ref[pl.ds(0, width // 2), cols(tile, part)] = dot_nn(own, grad_upper).astype(bf16)

        @pl.when(tile >= LAG)
        def _():
            join_end(tile - LAG)

        return carry

    lax.fori_loop(0, tiles, weigh_inner, 0)
    for tile in range(tiles - LAG, tiles):
        join_begin(tile)
        join_end(tile)
    for tile in range(tiles - STAGES, tiles):
        inner_part(tile).wait_send()
    for tile in (tiles - 2, tiles - 1):
        for copy in inner_stores(tile):
            copy.wait()
    own_out.wait()
    own_copy.wait()
    own_gout.wait()
    for m in range(4):
        for copy in (grad_copies[m] if m < 2 else []) + gate_copies[m]:
            copy.wait_send()
        for copy in out_copies[m] + copy_copies[m]:
            copy.wait()
    far_inner.wait_send()
    for copy in gout_copies:
        copy.wait()


ROW_ORDER = (0, 1, 2, 3)
BACK_COUNT = 2
STAGES = 4
LAG = 2


def run_experts(rows, gates, grads, far, inner, inner_others, outer):
    count, slots, width = rows.shape
    tokens = count * slots
    hidden = outer.shape[1]
    half = 256
    tiles = hidden // half
    shard = width // 8
    bf16 = jnp.bfloat16
    anywhere = pl.BlockSpec(memory_space=pl.ANY)
    sems = [pltpu.SemaphoreType.DMA((count,))] * 10 + [
        pltpu.SemaphoreType.DMA((12,)),
        pltpu.SemaphoreType.DMA((12,)),
        pltpu.SemaphoreType.DMA((2 * tiles,)),
        pltpu.SemaphoreType.DMA((2 * tiles,)),
        pltpu.SemaphoreType.DMA((3,)),
        pltpu.SemaphoreType.DMA((3,)),
        pltpu.SemaphoreType.DMA((10,)),
        pltpu.SemaphoreType.DMA((6,)),
    ]
    outs = pl.pallas_call(
        expert_kernel,
        out_shape=(
            jax.ShapeDtypeStruct(rows.shape, bf16),
            jax.ShapeDtypeStruct(rows.shape, bf16),
            jax.ShapeDtypeStruct(inner.shape, bf16),
            jax.ShapeDtypeStruct((4, tiles, half, shard), bf16),
            jax.ShapeDtypeStruct((tiles, 2, 4, shard, half), bf16),
        ),
        in_specs=[anywhere] * 8,
        out_specs=(anywhere,) * 5,
        scratch_shapes=[
            pltpu.VMEM((4, 4, slots, width), bf16),
            pltpu.VMEM((4, 2, shard, tokens), bf16),
            pltpu.VMEM((4, 4, slots, width), bf16),
            pltpu.VMEM((4, 4, 8, 128), jnp.float32),
            pltpu.VMEM((4, 2, shard, 2 * hidden), bf16),
            pltpu.VMEM((hidden, width), bf16),
            pltpu.VMEM((tokens, 2 * hidden), bf16),
            pltpu.VMEM((tokens, hidden), bf16),
            pltpu.VMEM((4, 4, slots, width), bf16),
            pltpu.VMEM((4, 4, slots, width), bf16),
            pltpu.VMEM((STAGES, 2, 4, shard, half), bf16),
            pltpu.VMEM((STAGES, 4, half, shard), bf16),
            pltpu.VMEM((2, 2, 4, shard, half), bf16),
            pltpu.VMEM((tiles, 4, half, shard), bf16),
        ] + sems,
        compiler_params=pltpu.CompilerParams(
            collective_id=1, has_side_effects=True, vmem_limit_bytes=63 * 2**20
        ),
        cost_estimate=pl.CostEstimate(
            flops=180 * 10**9, bytes_accessed=60 * 2**20, transcendentals=tokens * hidden
        ),
        name="run_experts",
    )(rows, gates, grads, far, inner, *inner_others, outer)
    return outs[0], outs[1], outs[2], outs[3].reshape(outer.shape)


def attend_back(pair, proj_ref, dout_ref, lse_ref, tile_ref, dproj_ref, span_ref, dk_ref, dv_ref, near_ref):
    length = proj_ref.shape[1]
    blocks = length // BLK
    depth = 64
    wide = 2 * depth
    here = slice(pair * wide, (pair + 1) * wide)
    lane = lax.broadcasted_iota(jnp.int32, (1, wide), 1)
    keys = proj_ref[1, :, here]
    values = proj_ref[2, :, here]
    keys_t = keys.T
    dk_ref[...] = jnp.zeros_like(dk_ref)
    dv_ref[...] = jnp.zeros_like(dv_ref)
    near_ref[...] = jnp.zeros_like(near_ref)
    far_sum = [jnp.zeros((1, BLK), jnp.float32) for h in range(2)]
    for block in range(blocks):
        rows = pl.ds(block * BLK, BLK)
        key_count = (block + 1) * BLK
        query = proj_ref[0, rows, here] * jnp.bfloat16(0.125)
        grad = dout_ref[rows, here]
        dq_parts = []
        dk_sum = None
        dv_sum = None
        for h in range(2):
            own = (lane // depth) == h
            query_h = jnp.where(own, query, jnp.bfloat16(0))
            grad_h = jnp.where(own, grad, jnp.bfloat16(0))
            scores = dot_nt(keys[:key_count], query_h)
            grad_p = dot_nt(values[:key_count], grad_h)
            lse = lse_ref[pair, h:h + 1, rows]
            far = tile_ref[2 * pair + h, 1, 0:1, BLK - 1:BLK].astype(jnp.float32)
            probs = []
            delta = None
            for kb in range(block + 1):
                d = block - kb
                part = scores[kb * BLK:(kb + 1) * BLK]
                bias = tile_ref[2 * pair + h, d].astype(jnp.float32) if d < 2 else far
                part = jnp.exp(part + (bias - lse))
                probs.append(part)
                term = jnp.sum(part * grad_p[kb * BLK:(kb + 1) * BLK], axis=0, keepdims=True)
                delta = term if delta is None else delta + term
            ds = []
            for kb in range(block + 1):
                d = block - kb
                part = probs[kb] * (grad_p[kb * BLK:(kb + 1) * BLK] - delta)
                if d < 2:
                    near_ref[h, d] += part
                else:
                    far_sum[h] = far_sum[h] + jnp.sum(part, axis=0, keepdims=True)
                ds.append(part.astype(jnp.bfloat16))
            ds = jnp.concatenate(ds, axis=0)
            weights = jnp.concatenate([p.astype(jnp.bfloat16) for p in probs], axis=0)
            dv_h = dot_nn(weights, grad_h)
            dk_h = dot_nn(ds, query_h)
            dv_sum = dv_h if dv_sum is None else dv_sum + dv_h
            dk_sum = dk_h if dk_sum is None else dk_sum + dk_h
            dq_parts.append(dot_nn(keys_t[h * depth:(h + 1) * depth, :key_count], ds))
        dk_ref[:key_count] += dk_sum
        dv_ref[:key_count] += dv_sum
        dproj_ref[0, rows, here] = (jnp.concatenate(dq_parts, axis=0).T * 0.125).astype(jnp.bfloat16)
    dproj_ref[1, :, here] = dk_ref[...].astype(jnp.bfloat16)
    dproj_ref[2, :, here] = dv_ref[...].astype(jnp.bfloat16)
    flip = (
        lax.broadcasted_iota(jnp.int32, (BLK, BLK), 0) + lax.broadcasted_iota(jnp.int32, (BLK, BLK), 1) == BLK - 1
    ).astype(jnp.bfloat16)
    lanes = lax.broadcasted_iota(jnp.int32, (1, 2 * BLK), 1)
    for h in range(2):
        for d in range(2):
            near = near_ref[h, d]
            near_high = near.astype(jnp.bfloat16)
            near_low = (near - near_high.astype(jnp.float32)).astype(jnp.bfloat16)
            flipped = dot_nn(flip, near_high) + dot_nn(flip, near_low)
            spread = jnp.concatenate([flipped, jnp.zeros((BLK, BLK), jnp.float32)], axis=1)
            turned = pltpu.roll(spread, 1, 1, stride=1, stride_axis=0)
            along = jnp.sum(turned, axis=0, keepdims=True)
            if d == 1:
                along = along + jnp.where(lanes == 2 * BLK - 1, jnp.sum(far_sum[h], axis=1, keepdims=True), 0.0)
            span_ref[2 * pair + h, d:d + 1, :] = along


def combine_kernel(
    returned_hbm, copies_hbm, hidden_hbm, cot_hbm, cols_hbm, wo_hbm, att_hbm, router_ref, gains_ref, counts_ref,
    mixed_ref, ghidden_ref, own_ref, other_ref, gout_ref, sums_ref,
    returned_ref, copies_ref, hidden_ref, cot_ref, cols_ref, wo_ref, att_ref, gp_ref, load_sem,
):
    f32, bf16 = jnp.float32, jnp.bfloat16
    rows, width = ghidden_ref.shape
    shard = width // 8
    experts = returned_ref.shape[0] // CAP
    loads = {}
    for name, source, target in (
        ("cols", cols_hbm, cols_ref), ("returned", returned_hbm, returned_ref), ("hidden", hidden_hbm, hidden_ref),
        ("cot", cot_hbm, cot_ref), ("copies", copies_hbm, copies_ref), ("wo", wo_hbm, wo_ref),
        ("att", att_hbm, att_ref),
    ):
        loads[name] = pltpu.make_async_copy(source, target, load_sem.at[len(loads)])
        loads[name].start()
    gain_second = gains_ref[1:2, :]
    router_t = router_ref[...]
    step = rows // 2
    counts = counts_ref[...]
    tokens = 32 * rows
    pairs_in_all = 2 * tokens
    push = loss_weight * experts * (counts / pairs_in_all) / tokens
    slot_lane = lax.broadcasted_iota(jnp.int32, (1, returned_ref.shape[0]), 1).astype(f32)
    expert_lane = lax.broadcasted_iota(jnp.int32, (1, shard), 1).astype(f32)
    gain2_sum = jnp.zeros((1, width), f32)
    route_sum = jnp.zeros((1, shard), f32)
    grad_router = jnp.zeros((shard, width), f32)
    for name in ("cols", "returned", "hidden", "cot"):
        loads[name].wait()
    for i in range(2):
        here = slice(i * step, (i + 1) * step)
        cols = cols_ref[here, :]
        route = jnp.where(expert_lane < experts, cols, 0.0)
        marks = [(slot_lane == cols[:, experts + 2 + c:experts + 3 + c]).astype(bf16) for c in range(2)]
        picked = [dot_nn(mark, returned_ref[...]) for mark in marks]
        hidden = hidden_ref[here, :]
        grad_mixed = cot_ref[here, :].astype(f32)
        mixed_ref[here, :] = (
            hidden + picked[0] * cols[:, experts:experts + 1] + picked[1] * cols[:, experts + 1:experts + 2]
        ).astype(bf16)
        grad_route = push
        for c in range(2):
            hit = expert_lane == cols[:, experts + 4 + c:experts + 5 + c]
            grad_route = grad_route + jnp.where(hit, jnp.sum(grad_mixed * picked[c], axis=1, keepdims=True), 0.0)
        grad_logits = route * (grad_route - jnp.sum(route * grad_route, axis=1, keepdims=True))
        route_sum = route_sum + jnp.sum(route, axis=0, keepdims=True)
        if i == 0:
            loads["copies"].wait()
        grad_second = dot_nn(marks[0] + marks[1], copies_ref[...]) + dot_nn(grad_logits.astype(bf16), router_t)
        normed, scale = normalize(hidden)
        second_norm = (normed * gain_second).astype(bf16)
        grad_router = grad_router + dot_nn(grad_logits.T.astype(bf16), second_norm)
        gain2_sum = gain2_sum + jnp.sum(grad_second * normed, axis=0, keepdims=True)
        grad_normed = grad_second * gain_second
        grad_hidden = grad_mixed + scale * (
            grad_normed - normed * jnp.mean(grad_normed * normed, axis=-1, keepdims=True)
        )
        ghidden_ref[here, :] = grad_hidden
        gp_ref[here, :] = grad_hidden.astype(bf16)


    loads["wo"].wait()
    own_width = own_ref.shape[1]
    other_ref[...] = dot_nt(gp_ref[...], wo_ref[own_width:, :]).astype(bf16)
    own_ref[...] = dot_nt(gp_ref[...], wo_ref[:own_width, :]).astype(bf16)
    loads["att"].wait()
    gout_ref[...] = dot_nn(att_ref[...].T, gp_ref[...]).astype(bf16)
    for owner in range(8):
        here = slice(owner * shard, (owner + 1) * shard)
        target = sums_ref.at[owner // 2, owner % 2]
        target[0:1, :] = jnp.zeros((1, shard), f32)
        target[1:2, :] = gain2_sum[:, here]
        target[2:2 + experts, :] = grad_router[:experts, here]
        target[18:22, :] = jnp.zeros((4, shard), f32)
        target[22:23, :] = route_sum
        target[23:24, :] = jnp.zeros((1, shard), f32)


def combine(returned, copies, hidden, cot, cols, wo, att, router_t, gains, counts):
    rows, width = hidden.shape
    shard = width // 8
    f32, bf16 = jnp.float32, jnp.bfloat16
    anywhere = pl.BlockSpec(memory_space=pl.ANY)
    inside = pl.BlockSpec(memory_space=pltpu.VMEM)
    held = (returned, copies, hidden, cot, cols, wo, att)
    return pl.pallas_call(
        combine_kernel,
        out_shape=(
            jax.ShapeDtypeStruct((rows, width), bf16),
            jax.ShapeDtypeStruct((rows, width), f32),
            jax.ShapeDtypeStruct((rows, width // 2), bf16),
            jax.ShapeDtypeStruct((rows, width // 2), bf16),
            jax.ShapeDtypeStruct((width, width), bf16),
            jax.ShapeDtypeStruct((4, 2, 24, shard), f32),
        ),
        in_specs=[anywhere] * 7 + [inside] * 3,
        out_specs=(inside,) * 6,
        scratch_shapes=[pltpu.VMEM(array.shape, array.dtype) for array in held]
        + [pltpu.VMEM((rows, width), bf16), pltpu.SemaphoreType.DMA((7,))],
        compiler_params=pltpu.CompilerParams(vmem_limit_bytes=48 * 2**20),
        cost_estimate=pl.CostEstimate(flops=8 * 10**9, bytes_accessed=20 * 2**20, transcendentals=0),
        name="combine",
    )(*held, router_t, gains, counts)


def back_kernel(
    own_hbm, other_hbm, gout_hbm, sums_hbm, ghidden_hbm, gains_ref, picks_ref, proj_hbm, lse_hbm, tile_hbm, wq_hbm,
    seq_hbm,
    gtok_ref, gqkv_ref, gwo_ref, sums_ref,
    ghidden_ref, proj_ref, lse_ref, tile_ref, wq_ref, seq_ref, dout_ref, dproj_ref, span_ref, dk_ref, dv_ref,
    near_ref, turned_ref, first_send_ref, first_in_ref,
    q_stage_ref, q_in_ref, q_own_ref, q_across_ref, q_z_ref, q_z_in_ref,
    gout_ref, o_in_ref, o_sum_ref, o_across_ref, o_z_ref, o_z_in_ref,
    s_own_ref, s_in_ref, s_sum_ref, s_across_ref, s_z_ref, s_z_in_ref,
    send_sem, recv_sem, load_sem,
):
    x, z, along_z, across, sibling = places()
    core = x % 2
    chip = x // 2
    half = z % 2
    f32, bf16 = jnp.float32, jnp.bfloat16
    rows, width = gtok_ref.shape
    shard = width // 8
    step = rows // 2
    group = gqkv_ref.shape[2]
    pair = (sibling, z)
    chips = [(device, z) for device in across]
    lines = [(x, other) for other in along_z]
    barrier = pltpu.get_barrier_semaphore()
    for peer in chips + lines + [pair]:
        pl.semaphore_signal(barrier, inc=1, device_id=peer, device_id_type=MESH_ID)
    loads = {}
    for name, source, target in (
        ("gout", gout_hbm, gout_ref), ("proj", proj_hbm, proj_ref),
        ("own", own_hbm, dout_ref.at[pl.ds(pl.multiple_of(half * rows, rows), rows), :]),
        ("other", other_hbm, dout_ref.at[pl.ds(pl.multiple_of((1 - half) * rows, rows), rows), :]),
        ("lse", lse_hbm, lse_ref), ("tile", tile_hbm, tile_ref), ("seq", seq_hbm, seq_ref), ("wq", wq_hbm, wq_ref),
        ("sums", sums_hbm, s_own_ref), ("ghidden", ghidden_hbm, ghidden_ref),
    ):
        loads[name] = pltpu.make_async_copy(source, target, load_sem.at[len(loads)])
        loads[name].start()
    pl.semaphore_wait(barrier, 7)
    started = []

    def send(source, target, device):
        index = len(started)
        copy = pltpu.make_async_remote_copy(
            src_ref=source, dst_ref=target, send_sem=send_sem.at[index], recv_sem=recv_sem.at[index],
            device_id=device, device_id_type=MESH_ID,
        )
        copy.start()
        started.append(copy)
        return copy

    def lanes_of(owner):
        return pl.ds(pl.multiple_of(owner * shard, shard), shard)

    loads["gout"].wait()
    o_pair = [send(gout_ref.at[:, lanes_of(2 * j + 1 - core)], o_in_ref.at[j], pair) for j in range(4)]

    gain_first = gains_ref[0:1, :]
    loads["seq"].wait()
    for i in range(4):
        normed, _ = normalize(seq_ref[i // 2, (i % 2) * step:(i % 2 + 1) * step, :].astype(f32))
        turned_ref[:, :, :, i * step:(i + 1) * step] = (
            (normed * gain_first).astype(bf16).T.reshape(4, 2, shard, step)
        )

    for name in ("proj", "lse", "tile", "own", "other"):
        loads[name].wait()

    def attend(number):
        attend_back(
            number, proj_ref, dout_ref, lse_ref, tile_ref, dproj_ref, span_ref, dk_ref, dv_ref, near_ref
        )

    def weigh_other(slot):
        here = pl.ds(slot * group, group)
        other = turned_ref[:, 1 - core].reshape(width // 2, 2 * rows)
        for c in range(3):
            q_stage_ref[slot, c] = dot_nn(other, dproj_ref[c, :, here]).astype(bf16).reshape(4, shard, group)
        return send(q_stage_ref.at[slot], q_in_ref.at[slot], pair)

    def weigh_own(slot):
        here = pl.ds(slot * group, group)
        own = turned_ref[:, core].reshape(width // 2, 2 * rows)
        for c in range(3):
            q_own_ref[slot, c] = dot_nn(own, dproj_ref[c, :, here]).astype(bf16).reshape(4, shard, group)

    def to_chips(slot, copy):
        copy.wait_recv()
        q_own_ref[slot] = (q_own_ref[slot].astype(f32) + q_in_ref[slot].astype(f32)).astype(bf16)
        return [
            send(q_own_ref.at[slot, :, device // 2], q_across_ref.at[slot, j], chips[j])
            for j, device in enumerate(across)
        ]

    def chip_total(slot, copies):
        for copy in copies:
            copy.wait_recv()
        total = q_own_ref[slot, :, chip].astype(f32)
        for j in range(3):
            total = total + q_across_ref[slot, j].astype(f32)
        return total

    attend(2)
    attend(3)
    q_pair_1 = weigh_other(1)
    for copy in o_pair:
        copy.wait_recv()
    for j in range(4):
        o_sum_ref[j] = (gout_ref[:, lanes_of(2 * j + core)].astype(f32) + o_in_ref[j].astype(f32)).astype(bf16)
    o_chips = [send(o_sum_ref.at[device // 2], o_across_ref.at[j], chips[j]) for j, device in enumerate(across)]
    weigh_own(1)
    q_chips_1 = to_chips(1, q_pair_1)
    attend(0)
    attend(1)

    loads["wq"].wait()
    gain1_sum = jnp.zeros((1, width), f32)
    for turn, side in enumerate((1 - half, half)):
        for i in range(2):
            here = pl.ds(pl.multiple_of(side * rows + i * step, step), step)
            part = (
                dot_nt(dproj_ref[0, here, :], wq_ref[0])
                + dot_nt(dproj_ref[1, here, :], wq_ref[1])
                + dot_nt(dproj_ref[2, here, :], wq_ref[2])
            )
            normed, _ = normalize(seq_ref[side, i * step:(i + 1) * step, :].astype(f32))
            gain1_sum = gain1_sum + jnp.sum(part * normed, axis=0, keepdims=True)
            if turn:
                gtok_ref[i * step:(i + 1) * step, :] = part
            else:
                first_send_ref[i * step:(i + 1) * step, :] = part.astype(bf16)
        if not turn:
            first_copy = send(first_send_ref, first_in_ref, lines[0])
            q_pair_0 = weigh_other(0)

    loads["sums"].wait()
    table = None
    for d in range(2):
        along = span_ref[:, d, :]
        high = along.astype(bf16)
        low = (along - high.astype(f32)).astype(bf16)
        part = dot_nn(high, picks_ref[d]) + dot_nn(low, picks_ref[d])
        table = part if table is None else table + part
    heads = table.shape[0] // 2
    table = table.T[:32, :]
    blank = jnp.zeros((table.shape[0], shard - heads), f32)
    placed = pltpu.roll(jnp.concatenate([table[:, :heads], blank], axis=1), heads * z, 1) + pltpu.roll(
        jnp.concatenate([table[:, heads:], blank], axis=1), heads * ((z + 2) % 4), 1
    )
    for owner in range(8):
        here = slice(owner * shard, (owner + 1) * shard)
        target = s_own_ref.at[owner // 2, owner % 2]
        target[0:1, :] = gain1_sum[:, here]
        target[18:22, :] = placed[4 * owner:4 * owner + 4, :]
    s_pair = send(s_own_ref.at[:, 1 - core], s_in_ref, pair)
    weigh_own(0)

    q_chips_0 = to_chips(0, q_pair_0)
    s_pair.wait_recv()
    s_sum_ref[...] = s_own_ref[:, core] + s_in_ref[...]
    s_chips = [send(s_sum_ref.at[device // 2], s_across_ref.at[j], chips[j]) for j, device in enumerate(across)]
    q_z_ref[...] = chip_total(1, q_chips_1).astype(bf16)
    q_line = send(q_z_ref, q_z_in_ref, lines[1])
    for copy in o_chips:
        copy.wait_recv()
    o_total = o_sum_ref[chip].astype(f32)
    for j in range(3):
        o_total = o_total + o_across_ref[j].astype(f32)
    rows_out = gwo_ref.shape[0]
    gwo_ref[...] = o_total[:rows_out]
    o_z_ref[...] = o_total[rows_out:].astype(bf16).reshape(o_z_ref.shape)
    out_slots = (2, 1, 3)
    o_lines = [send(o_z_ref.at[out_slots[j] - 1], o_z_in_ref.at[j], lines[j]) for j in range(3)]
    for copy in s_chips:
        copy.wait_recv()
    s_z_ref[...] = s_sum_ref[chip] + s_across_ref[0] + s_across_ref[1] + s_across_ref[2]
    s_lines = [send(s_z_ref, s_z_in_ref.at[j], lines[j]) for j in range(3)]
    gqkv_ref[...] = chip_total(0, q_chips_0)

    first_copy.wait_recv()
    loads["ghidden"].wait()
    for i in range(2):
        here = slice(i * step, (i + 1) * step)
        grad = (gtok_ref[here, :] + first_in_ref[here, :].astype(f32)) * gain_first
        normed, scale = normalize(seq_ref[half, here, :].astype(f32))
        gtok_ref[here, :] = ghidden_ref[here, :] + scale * (
            grad - normed * jnp.mean(grad * normed, axis=-1, keepdims=True)
        )
    q_line.wait_recv()
    gqkv_ref[...] += q_z_in_ref[...].astype(f32)
    for copy in s_lines + o_lines:
        copy.wait_recv()
    gwo_ref[...] += o_z_in_ref[0].astype(f32) + o_z_in_ref[1].astype(f32) + o_z_in_ref[2].astype(f32)
    sums = s_z_ref[...] + s_z_in_ref[0] + s_z_in_ref[1] + s_z_in_ref[2]
    sums_ref[...] = sums
    for copy in started:
        copy.wait_send()


def run_back(own, other, gout, sums, ghidden, gains, picks, proj, lse, tiles, wq, seq):
    rows, width = ghidden.shape
    length = 2 * rows
    shard = width // 8
    group = wq.shape[2] // 2
    rows_out = width // 4
    heads = tiles.shape[0]
    f32, bf16 = jnp.float32, jnp.bfloat16
    anywhere = pl.BlockSpec(memory_space=pl.ANY)
    inside = pl.BlockSpec(memory_space=pltpu.VMEM)
    copies_count = 4 + 2 + 3 + 3 + 3 + 1 + 1 + 3 + 1 + 3 + 3
    return pl.pallas_call(
        back_kernel,
        out_shape=(
            jax.ShapeDtypeStruct((rows, width), f32),
            jax.ShapeDtypeStruct((3, shard, group), f32),
            jax.ShapeDtypeStruct((rows_out, shard), f32),
            jax.ShapeDtypeStruct((24, shard), f32),
        ),
        in_specs=[anywhere] * 5 + [inside] * 2 + [anywhere] * 5,
        out_specs=(inside,) * 4,
        scratch_shapes=[
            pltpu.VMEM(ghidden.shape, f32),
            pltpu.VMEM(proj.shape, bf16),
            pltpu.VMEM(lse.shape, f32),
            pltpu.VMEM(tiles.shape, bf16),
            pltpu.VMEM(wq.shape, bf16),
            pltpu.VMEM(seq.shape, bf16),
            pltpu.VMEM((length, 2 * group), bf16),
            pltpu.VMEM(proj.shape, bf16),
            pltpu.VMEM((heads, 2, 2 * BLK), f32),
            pltpu.VMEM((length, 128), f32),
            pltpu.VMEM((length, 128), f32),
            pltpu.VMEM((2, 2, BLK, BLK), f32),
            pltpu.VMEM((4, 2, shard, length), bf16),
            pltpu.VMEM((rows, width), bf16),
            pltpu.VMEM((rows, width), bf16),
            pltpu.VMEM((2, 3, 4, shard, group), bf16),
            pltpu.VMEM((2, 3, 4, shard, group), bf16),
            pltpu.VMEM((2, 3, 4, shard, group), bf16),
            pltpu.VMEM((2, 3, 3, shard, group), bf16),
            pltpu.VMEM((3, shard, group), bf16),
            pltpu.VMEM((3, shard, group), bf16),
            pltpu.VMEM((width, width), bf16),
            pltpu.VMEM((4, width, shard), bf16),
            pltpu.VMEM((4, width, shard), bf16),
            pltpu.VMEM((3, width, shard), bf16),
            pltpu.VMEM((3, rows_out, shard), bf16),
            pltpu.VMEM((3, rows_out, shard), bf16),
            pltpu.VMEM((4, 2, 24, shard), f32),
            pltpu.VMEM((4, 24, shard), f32),
            pltpu.VMEM((4, 24, shard), f32),
            pltpu.VMEM((3, 24, shard), f32),
            pltpu.VMEM((24, shard), f32),
            pltpu.VMEM((3, 24, shard), f32),
            pltpu.SemaphoreType.DMA((copies_count,)),
            pltpu.SemaphoreType.DMA((copies_count,)),
            pltpu.SemaphoreType.DMA((10,)),
        ],
        compiler_params=pltpu.CompilerParams(
            collective_id=2, has_side_effects=True, vmem_limit_bytes=60 * 2**20
        ),
        cost_estimate=pl.CostEstimate(flops=60 * 10**9, bytes_accessed=60 * 2**20, transcendentals=0),
        name="run_back",
    )(own, other, gout, sums, ghidden, gains, picks, proj, lse, tiles, wq, seq)


def final_kernel(
    ginner_hbm, gtok_hbm, gqkv_hbm, gwo_hbm, sums_ref, counts_ref,
    inner_hbm, tok_hbm, qkv_hbm, wo_hbm, gain1_ref, gain2_ref, grouter_ref, gbias_ref, load_ref, loss_ref,
    in_ref, out_ref, in_sem, out_sem, copy_sem,
):
    z = lax.axis_index("gy")
    f32 = jnp.float32
    copies = [
        pltpu.make_async_copy(source, target, copy_sem.at[n])
        for n, (source, target) in enumerate(((gtok_hbm, tok_hbm), (gqkv_hbm, qkv_hbm), (gwo_hbm, wo_hbm)))
    ]
    depth, _, wide = in_ref.shape
    blocks = [
        (n, pl.ds(part * wide, wide)) for n in range(ginner_hbm.shape[0]) for part in range(ginner_hbm.shape[2] // wide)
    ]
    loads = [
        pltpu.make_async_copy(ginner_hbm.at[n, :, here], in_ref.at[i % depth], in_sem.at[i % depth])
        for i, (n, here) in enumerate(blocks)
    ]
    stores = [
        pltpu.make_async_copy(out_ref.at[i % depth], inner_hbm.at[n, :, here], out_sem.at[i % depth])
        for i, (n, here) in enumerate(blocks)
    ]
    for i in range(depth - 1):
        loads[i].start()
    for copy in copies:
        copy.start()
    experts = load_ref.shape[1]
    heads = gbias_ref.shape[1]
    shard = sums_ref.shape[1]
    sums = sums_ref[...]
    gain1_ref[...] = sums[0:1, :]
    gain2_ref[...] = sums[1:2, :]
    grouter_ref[...] = sums[2:2 + experts, :].T
    gbias_ref[...] = pltpu.roll(sums[16:24, :], (shard - heads * z) % shard, 1)[2:6, :heads]
    tokens = 32 * gtok_hbm.shape[0]
    counts = counts_ref[:, :experts]
    pairs_in_all = 2 * tokens
    prob_sums = sums[22:23, :experts]
    load_ref[...] = jnp.concatenate([experts * counts / pairs_in_all, experts * prob_sums / tokens], axis=0)
    loss_ref[...] = experts * jnp.sum(counts / pairs_in_all * (prob_sums / tokens), axis=1, keepdims=True)
    for i in range(len(blocks)):
        if i + depth - 1 < len(blocks):
            loads[i + depth - 1].start()
        loads[i].wait()
        if i >= depth:
            stores[i - depth].wait()
        out_ref[i % depth] = in_ref[i % depth].astype(f32)
        stores[i].start()
    for store in stores[-depth:]:
        store.wait()
    for copy in copies:
        copy.wait()


def finish(ginner, gtok, gqkv, gwo, sums, counts, experts, heads):
    f32, bf16 = jnp.float32, jnp.bfloat16
    local, shard, inner_width = ginner.shape
    wide = inner_width // 4
    anywhere = pl.BlockSpec(memory_space=pl.ANY)
    inside = pl.BlockSpec(memory_space=pltpu.VMEM)
    return pl.pallas_call(
        final_kernel,
        out_shape=(
            jax.ShapeDtypeStruct(ginner.shape, f32),
            jax.ShapeDtypeStruct(gtok.shape, f32),
            jax.ShapeDtypeStruct(gqkv.shape, f32),
            jax.ShapeDtypeStruct(gwo.shape, f32),
            jax.ShapeDtypeStruct((1, shard), f32),
            jax.ShapeDtypeStruct((1, shard), f32),
            jax.ShapeDtypeStruct((shard, experts), f32),
            jax.ShapeDtypeStruct((4, heads), f32),
            jax.ShapeDtypeStruct((2, experts), f32),
            jax.ShapeDtypeStruct((1, 1), f32),
        ),
        in_specs=[anywhere] * 4 + [inside] * 2,
        out_specs=(anywhere,) * 4 + (inside,) * 6,
        scratch_shapes=[
            pltpu.VMEM((4, shard, wide), bf16),
            pltpu.VMEM((4, shard, wide), f32),
            pltpu.SemaphoreType.DMA((4,)),
            pltpu.SemaphoreType.DMA((4,)),
            pltpu.SemaphoreType.DMA((3,)),
        ],
        compiler_params=pltpu.CompilerParams(vmem_limit_bytes=32 * 2**20),
        cost_estimate=pl.CostEstimate(flops=0, bytes_accessed=24 * 2**20, transcendentals=0),
        name="finish",
    )(ginner, gtok, gqkv, gwo, sums, counts)


def fast_device(
    tokens, expert_ids, gain_attn, w_qkv, w_out, rel_bias, gain_ffn, router, w_in, w_down, cotangent
):
    f32, bf16 = jnp.float32, jnp.bfloat16
    tok_dev, model_width = tokens.shape
    expert_count = router.shape[1]
    top_count = expert_ids.shape[1]
    shard = model_width // 8
    group_heads = rel_bias.shape[1]

    expert_row = jnp.arange(expert_count, dtype=jnp.int32)
    hits = [(expert_ids[:, c][:, None] == expert_row[None]) for c in range(top_count)]
    both = sum(hit.astype(bf16) for hit in hits)
    steps = jnp.arange(tok_dev, dtype=jnp.int32)
    lower = (steps[None, :] < steps[:, None]).astype(bf16)
    before = jnp.dot(lower, both, preferred_element_type=f32)
    slots = [jnp.sum(jnp.where(hit, before, 0.0), axis=1).astype(jnp.int32) for hit in hits]
    kept = [slot < CAP for slot in slots]
    local_counts = jnp.sum(both.astype(f32), axis=0)
    count_high = jnp.floor(local_counts / 32.0)
    count_low = local_counts - 32.0 * count_high

    def lanes(rows):
        return jnp.pad(rows.astype(bf16), ((0, 0), (0, shard - rows.shape[1])))

    small = jnp.concatenate(
        [
            router.T,
            gain_attn[None],
            gain_ffn[None],
            lanes(rel_bias),
            lanes(count_high[None]),
            lanes(count_low[None]),
            jnp.zeros((8, shard), bf16),
        ],
        axis=0,
    )
    spots = [
        jnp.where(keep, ((expert_ids[:, c] % 4) * 4 + expert_ids[:, c] // 4) * CAP + slots[c], -1)
        for c, keep in enumerate(kept)
    ]
    buffer_rows = jnp.arange(expert_count * CAP, dtype=jnp.int32)
    marks = [buffer_rows[:, None] == spot[None] for spot in spots]
    dispatch = (marks[0] | marks[1]).astype(bf16)
    grad_rows = jnp.dot(dispatch, cotangent, preferred_element_type=f32).astype(bf16)
    grad_rows = grad_rows.reshape(expert_count, CAP, model_width)

    buckets = span_buckets()[:, :, None] == jnp.arange(128, dtype=jnp.int32)
    picks = buckets.astype(bf16)
    (
        seq_tokens, qkv_weight, out_weight, smalls, projected, attended, log_totals, bias_tiles, inner_a, inner_b,
        grads_far,
    ) = run_front(tokens, w_qkv, w_out, small, w_in, grad_rows, picks)

    own_small = smalls[0]
    router_t = own_small[:, :16].transpose(1, 0, 2).reshape(expert_count, model_width)
    gain_first = own_small[:, 16].reshape(model_width).astype(f32)
    gain_second = own_small[:, 17].reshape(model_width).astype(f32)
    all_counts = smalls[:, :, 22:24, :expert_count].astype(f32).sum(axis=(0, 1))
    counts = 32.0 * all_counts[0] + all_counts[1]

    hidden_state = tokens.astype(f32) + jnp.dot(attended, out_weight, preferred_element_type=f32)
    normed_two, _ = normalize(hidden_state)
    second_norm = (normed_two * gain_second).astype(bf16)
    logits = lax.dot_general(second_norm, router_t, (((1,), (1,)), ((), ())), preferred_element_type=f32)
    route = jax.nn.softmax(logits, axis=-1)

    gates = [
        jnp.where(keep, jnp.sum(jnp.where(hit, route, 0.0), axis=1), 0.0) for hit, keep in zip(hits, kept)
    ]
    gate_rows = jnp.sum(
        jnp.where(marks[0], gates[0][None], 0.0) + jnp.where(marks[1], gates[1][None], 0.0), axis=1
    )
    send_rows = jnp.dot(dispatch, second_norm, preferred_element_type=f32).astype(bf16)
    gate_rows = jnp.pad(gate_rows.reshape(expert_count, 1, CAP), ((0, 0), (0, 7), (0, 128 - CAP)))
    returned, grad_copies, grad_inner, grad_outer = run_experts(
        send_rows.reshape(expert_count, CAP, model_width),
        gate_rows,
        grad_rows,
        grads_far,
        w_in,
        (inner_a, inner_b),
        w_down,
    )
    grad_inner = exchange_chips(grad_inner)
    columns = jnp.concatenate(
        [route] + [column.astype(f32)[:, None] for column in gates + spots + [expert_ids[:, 0], expert_ids[:, 1]]],
        axis=1,
    )
    gains = jnp.stack([gain_first, gain_second])
    count_row = jnp.pad(counts, (0, 128 - expert_count))[None]
    mixed, grad_hidden, grad_own, grad_other, grad_out_weight, sums = combine(
        returned.reshape(-1, model_width),
        grad_copies.reshape(-1, model_width),
        hidden_state,
        cotangent,
        jnp.pad(columns, ((0, 0), (0, 128 - columns.shape[1]))),
        out_weight,
        attended,
        jnp.pad(router_t, ((0, 128 - expert_count), (0, 0))),
        gains,
        count_row,
    )
    grad_other, grad_outer = lax.optimization_barrier((swap_z(grad_other, 1), grad_outer.astype(f32)))
    grad_tokens, grad_qkv, grad_out_weight, sums = run_back(
        grad_own,
        grad_other,
        grad_out_weight,
        sums,
        grad_hidden,
        gains,
        picks,
        projected,
        log_totals,
        bias_tiles,
        qkv_weight,
        seq_tokens,
    )
    (
        grad_inner, grad_tokens, grad_qkv, grad_out_weight, gain_one, gain_two, grad_router, grad_rel_bias, router_load,
        loss,
    ) = finish(
        grad_inner, grad_tokens, grad_qkv, grad_out_weight, sums, count_row, expert_count, group_heads
    )
    return (
        mixed,
        loss[0, 0],
        router_load,
        grad_tokens,
        gain_one[0],
        grad_qkv,
        grad_out_weight,
        grad_rel_bias,
        gain_two[0],
        grad_router,
        grad_inner,
        grad_outer,
    )


def solution(mesh):
    in_specs = (
        P(("gx", "gy"), None),
        P(("gx", "gy"), None),
        P("gx"),
        P(None, "gx", "gy"),
        P("gy", "gx"),
        P("gx", "gy"),
        P("gx"),
        P("gx", None),
        P("gy", "gx", None),
        P("gy", None, "gx"),
        P(("gx", "gy"), None),
    )
    out_specs = (
        P(("gx", "gy"), None),
        P(),
        P(),
        P(("gx", "gy"), None),
        P("gx"),
        P(None, "gx", "gy"),
        P("gy", "gx"),
        P("gx", "gy"),
        P("gx"),
        P("gx", None),
        P("gy", "gx", None),
        P("gy", None, "gx"),
    )
    return jax.shard_map(
        fast_device if fits_fast(mesh) else general_device, mesh=mesh, in_specs=in_specs, out_specs=out_specs, check_vma=False
    )
```

profile of v0, /device:TPU:0, one launch (start us, length us, event | category | flops | bytes accessed | tf_op | source)
XLA Modules:
  0.0 504.8 jit_solution(16866178900379492600)
XLA Ops:
  0.7 0.8 fusion.58
  1.4 0.3 select_reduce_fusion.3
  1.7 0.7 pad.27
  2.4 0.9 fusion.8.picks_ref
  3.4 0.0 copy-start.24
  3.4 0.0 copy-start.25
  3.4 0.0 copy-start.26
  3.4 4.3 convolution_convert_fusion.1
  7.7 0.0 copy-done.24
  7.7 0.0 copy-done.25
  7.7 0.0 copy-done.26
  7.7 1.8 concatenate.6.small_ref
  9.5 108.9 %run_front.1 = (bf16[2,512,1024]{2,1,0:T(8,128)(2,1)}, bf16[3,1024,512]{2,1,0:T(8,128)(2,1)}, bf16[1024,1024]{1,0:T(8,128)(2,1)}, bf16[4,8,32,128]{3,2,1,0:T(8,1...) custom-call(bf16[512,1024]{1,0:T(8,128)(2,1)} %tok_ref.1, ...), custom_call_target="tpu_custom_call" | custom-call | flops 60000002048 | bytes 31457280 | tf_op jit(solution)/shard_map/run_front/pallas_call | solution.py:657
  118.4 0.8 slice_bitcast_fusion
  119.2 0.6 slice_bitcast_fusion.2
  119.9 0.0 copy-done.27
  119.9 3.3 multiply_reduce_fusion
  123.2 3.2 convolution_convert_fusion
  126.4 0.0 copy-done.12
  126.4 0.0 copy-done.11
  126.4 0.5 fusion.61
  126.9 0.6 select_reduce_fusion.1
  127.5 0.6 fusion.59
  128.1 0.6 fusion.60
  128.7 0.0 copy-done.15
  128.7 0.0 copy-done.17
  128.7 0.6 add_reduce_fusion
  129.3 0.1 reshape.467
  129.4 0.6 pad.30.gates_ref
  130.0 239.3 %run_experts.1 = (bf16[16,80,1024]{2,1,0:T(8,128)(2,1)}, bf16[16,80,1024]{2,1,0:T(8,128)(2,1)}, bf16[4,128,5632]{2,1,0:T(8,128)(2,1)}, bf16[4,11,256,128]{3,2,1,0:T(8,128)(2,1)}, bf16[11,2,4,128,256]{4,3,2,1,0:T(8,128)(2,1)}) custom-call(bf16[16,80,1024]{2,1,0:T(8,128)(2,1)} %bitcast.78, f32[16,8,128]{2,1,0:T(8,128)} %pad.30.gates_ref, ...), custom_call_target="tpu_custom_call" | custom-call | flops 179999997952 | bytes 62914560 | tf_op jit(solution)/shard_map/run_experts/pallas_call | solution.py:1086
  369.3 0.0 copy-start.13
  369.4 0.0 copy-start.18
  369.4 0.0 copy-start.20
  369.4 0.0 copy-start.19
  369.4 0.0 copy-start.23
  369.4 0.0 copy-start.16
  369.4 0.0 copy-start.21
  369.4 0.0 copy-start.22
  369.4 0.0 copy-start.5
  369.5 5.3 %all-to-all-start = ((bf16[4,128,5632]{2,1,0:T(8,128)(2,1)}), bf16[4,128,5632]{2,1,0:T(8,128)(2,1)}, u32[]{:S(2)}, u32[]{:S(2)}) async-start(bf16[4,128,5632]{2,1,0:T(8,128)(2,1)} %get-tuple-element.58), calls=%async_computation | async-start | bytes 11534336 | tf_op jit(solution)/shard_map/all_to_all | solution.py:703
  374.8 0.9 convert_reduce_fusion
  375.7 0.0 copy-done.20
  375.8 0.0 copy-done.16
  375.8 0.1 copy.47
  376.1 0.0 copy-start.4
  376.1 0.0 copy-done.5
  376.1 0.0 copy-done.6
  376.1 0.0 copy-start.10
  376.1 12.8 %combine.1 = (bf16[512,1024]{1,0:T(8,128)(2,1)}, f32[512,1024]{1,0:T(8,128)S(1)}, bf16[512,512]{1,0:T(8,128)(2,1)S(1)}, bf16[512,512]{1,0:T(8,128)(2,1)S(1)}, bf...) custom-call(bf16[1280,1024]{1,0:T(8,128)(2,1)} %bitcast.76, bf16[1280,1024]{1,0:T(8,128)(2,1)} %bitcast.77, ...), custom_call_target="tpu_custom_call" | custom-call | flops 8000000000 | bytes 20971520 | tf_op jit(solution)/shard_map/combine/pallas_call | solution.py:1290
  389.0 0.0 copy-done.4
  389.0 0.0 copy-start.7
  389.0 0.0 copy-start.9
  389.0 14.3 %collective-permute-start = (bf16[512,512]{1,0:T(8,128)(2,1)S(1)}, bf16[512,512]{1,0:T(8,128)(2,1)S(1)}, u32[]{:S(2)}, u32[]{:S(2)}) collective-permute-start(bf16[512,512]{1,0:T(8,128)(2,1)S(1)} %get-tuple-element.60), channel_id=1, source_target_pairs={{0,1},{1,0},{2,3},{3,2},{4,5},{5,4},{6,7},{7,6},{8,9},{9,8},{10,11... | collective-permute-start | bytes 1572872 | tf_op jit(solution)/shard_map/ppermute | solution.py:698
  403.3 3.1 bitcast_convert_fusion
  406.4 8.8 %collective-permute-done.other_hbm = bf16[512,512]{1,0:T(8,128)(2,1)S(1)} collective-permute-done((bf16[512,512]{1,0:T(8,128)(2,1)S(1)}, bf16[512,512]{1,0:T(8,128)(2,1)S(1)}, u32[]{:S(2)}, u32[]{:S(2)}) %collective-permute-start) | collective-permute-done | bytes 524320 | tf_op jit(solution)/shard_map/ppermute | solution.py:698
  415.2 0.8 copy-done.28
  416.0 75.3 %run_back.1 = (f32[512,1024]{1,0:T(8,128)}, f32[3,128,256]{2,1,0:T(8,128)}, f32[256,128]{1,0:T(8,128)}, f32[24,128]{1,0:T(8,128)}) custom-call(bf16[512,512]{1,0:T(8,128)(2,1)} %copy-done.8, bf16[512,512]{1,0:T(8,128)(2,1)} %copy-done.28, bf16[1024,1024]{1,0:T(8,128)(2,1)} %get-tuple-element.63.gout_hbm, f32[4,2,24,128]{3,2,1,0:T(8,128)} %copy-done.9, ...), custom_call_target="tpu_custom_call" | custom-call | flops 60000002048 | bytes 62914560 | tf_op jit(solution)/shard_map/run_back/pallas_call | solution.py:1518
  491.3 0.0 all-to-all-done.ginner_hbm
  491.3 1.6 copy-done
  492.9 1.0 copy-done.1
  493.9 0.9 copy-done.2
  494.8 0.7 copy-done.3
  495.5 8.2 %finish.1 = (f32[4,128,5632]{2,1,0:T(8,128)}, f32[512,1024]{1,0:T(8,128)}, f32[3,128,256]{2,1,0:T(8,128)}, f32[256,128]{1,0:T(8,128)}, f32[1,128]{1,0:T(1,128)},...) custom-call(bf16[4,128,5632]{2,1,0:T(8,128)(2,1)} %all-to-all-done.ginner_h, ...), custom_call_target="tpu_custom_call" | custom-call | bytes 25165824 | tf_op jit(solution)/shard_map/finish/pallas_call | solution.py:1635
  503.7 0.7 copy.48
  (43 shorter events, 0.3 us)
Async XLA Ops:
  3.4 4.3 copy-start.24
  3.4 4.3 copy-start.25
  3.4 4.3 copy-start.26
  9.5 110.4 %copy-start.27 = (bf16[512,1024]{1,0:T(8,128)(2,1)S(1)}, bf16[512,1024]{1,0:T(8,128)(2,1)}, u32[]{:S(2)}) copy-start(bf16[512,1024]{1,0:T(8,128)(2,1)} %tok_ref.1) | copy-start | bytes 3145732
  119.2 7.1 %copy-start.12 = (bf16[8,32,128]{2,1,0:T(8,128)(2,1)}, bf16[8,32,128]{2,1,0:T(8,128)(2,1)S(1)}, u32[]{:S(2)}) copy-start(bf16[8,32,128]{2,1,0:T(8,128)(2,1)S(1)} %slice_bitcast_fusion) | copy-start | bytes 196612
  123.1 3.2 copy-start.11
  127.5 1.2 copy-start.15
  127.5 1.2 copy-start.17
  369.3 5.4 %copy-start.13 = (bf16[8,32,128]{2,1,0:T(8,128)(2,1)S(1)}, bf16[8,32,128]{2,1,0:T(8,128)(2,1)}, u32[]{:S(2)}) copy-start(bf16[8,32,128]{2,1,0:T(8,128)(2,1)} %copy-done.12) | copy-start | bytes 196612
  369.4 6.3 %copy-start.18 = (f32[512]{0:T(512)S(1)}, f32[512]{0:T(512)}, u32[]{:S(2)}) copy-start(f32[512]{0:T(512)} %copy-done.17) | copy-start | bytes 6148
  369.4 6.3 %copy-start.20 = (s32[512]{0:T(512)S(1)}, s32[512]{0:T(512)}, u32[]{:S(2)}) copy-start(s32[512]{0:T(512)} %get-tuple-element.151) | copy-start | bytes 6148
  369.4 6.3 %copy-start.19 = (s32[512]{0:T(512)S(1)}, s32[512]{0:T(512)}, u32[]{:S(2)}) copy-start(s32[512]{0:T(512)} %get-tuple-element.149) | copy-start | bytes 6148
  369.4 6.3 %copy-start.23 = (s32[512,2]{0,1:T(2,128)S(1)}, s32[512,2]{0,1:T(2,128)}, u32[]{:S(2)}) copy-start(s32[512,2]{0,1:T(2,128)} %param.12) | copy-start | bytes 12292
  369.4 6.4 %copy-start.16 = (f32[512]{0:T(512)S(1)}, f32[512]{0:T(512)}, u32[]{:S(2)}) copy-start(f32[512]{0:T(512)} %copy-done.15) | copy-start | bytes 6148
  369.4 6.4 %copy-start.14 = (f32[512,16]{0,1:T(8,128)S(1)}, f32[512,16]{0,1:T(8,128)}, u32[]{:S(2)}) copy-start(f32[512,16]{0,1:T(8,128)} %get-tuple-element.139) | copy-start | bytes 98308
  369.4 6.6 %copy-start.21 = (bf16[1,1024]{1,0:T(2,128)(2,1)S(1)}, bf16[1,1024]{1,0:T(2,128)(2,1)}, u32[]{:S(2)}) copy-start(bf16[1,1024]{1,0:T(2,128)(2,1)} %get-tuple-element.140) | copy-start | bytes 6148
  369.4 6.6 %copy-start.22 = (bf16[1,1024]{1,0:T(2,128)(2,1)S(1)}, bf16[1,1024]{1,0:T(2,128)(2,1)}, u32[]{:S(2)}) copy-start(bf16[1,1024]{1,0:T(2,128)(2,1)} %get-tuple-element.141) | copy-start | bytes 6148
  369.4 6.7 %copy-start.5 = (bf16[512,1024]{1,0:T(8,128)(2,1)S(1)}, bf16[512,1024]{1,0:T(8,128)(2,1)}, u32[]{:S(2)}) copy-start(bf16[512,1024]{1,0:T(8,128)(2,1)} %cot_hbm.1) | copy-start | bytes 3145732
  369.5 6.7 %copy-start.6 = (bf16[512,1024]{1,0:T(8,128)(2,1)S(1)}, bf16[512,1024]{1,0:T(8,128)(2,1)}, u32[]{:S(2)}) copy-start(bf16[512,1024]{1,0:T(8,128)(2,1)} %get-tuple-element.49.att_hbm) | copy-start | bytes 3145732
  369.5 121.9 %all-to-all-start = ((bf16[4,128,5632]{2,1,0:T(8,128)(2,1)}), bf16[4,128,5632]{2,1,0:T(8,128)(2,1)}, u32[]{:S(2)}, u32[]{:S(2)}) async-start(bf16[4,128,5632]{2,1,0:T(8,128)(2,1)} %get-tuple-element.58), calls=%async_computation | async-start | bytes 11534336 | tf_op jit(solution)/shard_map/all_to_all | solution.py:703
  376.1 12.9 %copy-start.4 = (f32[2,1024]{1,0:T(2,128)}, f32[2,1024]{1,0:T(2,128)S(1)}, u32[]{:S(2)}) copy-start(f32[2,1024]{1,0:T(2,128)S(1)} %maximum_convert_fusion.gains_ref) | copy-start | bytes 24580
  376.1 27.2 %copy-start.10 = (bf16[4,11,256,128]{3,2,1,0:T(8,128)(2,1)S(1)}, bf16[4,11,256,128]{3,2,1,0:T(8,128)(2,1)}, u32[]{:S(2)}) copy-start(bf16[4,11,256,128]{3,2,1,0:T(8,128)(2,1)} %get-tuple-element.61) | copy-start | bytes 8650756
  389.0 17.4 %copy-start.7 = (f32[512,1024]{1,0:T(8,128)}, f32[512,1024]{1,0:T(8,128)S(1)}, u32[]{:S(2)}) copy-start(f32[512,1024]{1,0:T(8,128)S(1)} %get-tuple-element.65.ghidden_hbm) | copy-start | bytes 6291460
  389.0 17.4 %copy-start.8 = (bf16[512,512]{1,0:T(8,128)(2,1)}, bf16[512,512]{1,0:T(8,128)(2,1)S(1)}, u32[]{:S(2)}) copy-start(bf16[512,512]{1,0:T(8,128)(2,1)S(1)} %get-tuple-element.59.own_hbm) | copy-start | bytes 1572868
  389.0 17.4 %copy-start.9 = (f32[4,2,24,128]{3,2,1,0:T(8,128)}, f32[4,2,24,128]{3,2,1,0:T(8,128)S(1)}, u32[]{:S(2)}) copy-start(f32[4,2,24,128]{3,2,1,0:T(8,128)S(1)} %get-tuple-element.64.sums_hbm) | copy-start | bytes 294916
  389.0 26.2 %collective-permute-start = (bf16[512,512]{1,0:T(8,128)(2,1)S(1)}, bf16[512,512]{1,0:T(8,128)(2,1)S(1)}, u32[]{:S(2)}, u32[]{:S(2)}) collective-permute-start(bf16[512,512]{1,0:T(8,128)(2,1)S(1)} %get-tuple-element.60), channel_id=1, source_target_pairs={{0,1},{1,0},{2,3},{3,2},{4,5},{5,4},{6,7},{7,6},{8,9},{9,8},{10,11... | collective-permute-start | bytes 1572872 | tf_op jit(solution)/shard_map/ppermute | solution.py:698
  415.2 0.8 copy-start.28
  491.3 1.6 copy-start
  492.9 1.0 copy-start.1
  493.9 0.9 copy-start.2
  494.8 0.7 copy-start.3
where the time goes:
time: 514 us; the launch traced here: 505 us
  Pallas kernels  445 us (87%)
  starting transfers between devices  19.6 us (4%)
  matrix products  11.5 us (2%)
  local copies, waits for them, and re-layouts  10.8 us (2%)
  waiting for transfers between devices  8.78 us (2%)
  other arithmetic  8.08 us (2%)
    pallas_call x1, Pallas kernels, run_experts(): pl.pallas_call(expert_kernel, out_shape=(jax.ShapeDtypeStruct(rows.shape,...  239 us
    pallas_call x1, Pallas kernels, run_front(): pl.pallas_call(front_kernel, out_shape=(jax.ShapeDtypeStruct(seq, bf16),...  109 us
    pallas_call x1, Pallas kernels, run_back(): pl.pallas_call(back_kernel, out_shape=(jax.ShapeDtypeStruct((rows, width)...  75.3 us
    ppermute x1, starting transfers between devices, swap_z(): return lax.ppermute(values, 'gy', [(i, i ^ step) for i in range(4)])  14.3 us
    pallas_call x1, Pallas kernels, combine(): pl.pallas_call(combine_kernel, out_shape=(jax.ShapeDtypeStruct((rows, wid...  12.8 us
  transfers between devices with their start and end apart: 2, of which 1 were waited for; matrix products, arithmetic and copies ran while one was open for 1% of the time, Pallas kernels for 17%

commit v1 on v0

--- a/solution.py
+++ b/solution.py
@@ -475,9 +475,9 @@
 
 
 def front_kernel(
-    tok_ref, wq_ref, wo_ref, small_ref, inner_ref, grads_ref, picks_ref,
-    seq_out, wqs_out, wos_out, smalls_out, proj_ref, att_ref, lse_ref, kept_ref, inner_a_ref, inner_b_ref, far_ref,
-    seq_ref, wqs_ref, wos_ref, smalls_ref, normed_ref, attended_ref, got_ref, span_ref, tile_ref,
+    tok_ref, wq_ref, wo_ref, small_ref, inner_ref, cot_hbm, picks_ref, ids_ref, spots_ref,
+    seq_out, wqs_out, wos_out, smalls_out, proj_ref, att_ref, lse_ref, kept_ref, hidden_ref, cols_ref, gates_ref, rows_hbm, grads_hbm, inner_a_ref, inner_b_ref, inner_c_ref, far_ref,
+    seq_ref, wqs_ref, wos_ref, wos_in_ref, smalls_ref, normed_ref, attended_ref, got_ref, span_ref, tile_ref, cot_ref, grads_ref, rows_ref, second_ref, gate_parts_ref,
     send_sem, recv_sem, local_sem, out_sem,
 ):
     x, z, along_z, across, sibling = places()
@@ -495,18 +495,16 @@
     rows, width = tok_ref.shape
 
     def qkv_part(owner, slot):
-        return wqs_ref.at[:, pl.ds(pl.multiple_of(owner * depth, depth), depth), pl.ds(slot * group, group)]
+        return wqs_ref.at[slot, owner]
 
     def out_part(owner, slot, slots):
-        return wos_ref.at[
-            pl.ds(slot * rows_out, slots * rows_out), pl.ds(pl.multiple_of(owner * depth, depth), depth)
-        ]
+        return wos_in_ref.at[owner, pl.ds(slot * rows_out, slots * rows_out), :]
 
     keeps = [
         pltpu.make_async_copy(source, target, local_sem.at[n])
         for n, (source, target) in enumerate(
             ((small_ref, smalls_ref.at[0, x]), (wo_ref, out_part(x, 0, 1)), (wq_ref, qkv_part(x, 0)),
-             (tok_ref, seq_ref.at[half]))
+             (tok_ref, seq_ref.at[half]), (cot_hbm, cot_ref))
         )
     ]
     for copy in keeps:
@@ -531,6 +529,20 @@
     wq_first = [send(wq_ref, qkv_part(x, 0), (other, z)) for other in near]
     tok_z = send(tok_ref, seq_ref.at[half], (x, along_z[0]))
     wo_z = [send(wo_ref, out_part(x, out_slots[j], 1), (x, along_z[j])) for j in range(3)]
+    blocks = rows_ref.shape[0] // 4
+    slots = rows_ref.shape[1]
+    chunk = blocks * slots
+    slot_row = lax.broadcasted_iota(jnp.int32, (chunk, 1), 0).astype(f32)
+
+    def marks(i):
+        return [(slot_row + i * chunk == spots_ref[c:c + 1, :]).astype(bf16) for c in range(2)]
+
+    keeps[4].wait()
+    for i in range(4):
+        first, second = marks(i)
+        grads_ref[i * blocks:(i + 1) * blocks] = (
+            dot_nn(first + second, cot_ref[...]).astype(bf16).reshape(blocks, slots, width)
+        )
     keeps[0].wait()
     for copy in small_z:
         copy.wait_recv()
@@ -551,11 +563,11 @@
         first_on.append(send(qkv_part(owner, 0), qkv_part(owner, 0), (sibling, z)))
     for copy in [small_x[3], wq_first[3]] + small_on + first_on:
         copy.wait_recv()
-    for copy in keeps[1:]:
+    for copy in keeps[1:4]:
         copy.wait()
     inner_copies = [
         send(inner_ref.at[device // 2], target, (device, z))
-        for device, target in zip(across[:2], (inner_a_ref, inner_b_ref))
+        for device, target in zip(across, (inner_a_ref, inner_b_ref, inner_c_ref))
     ]
 
     own_smalls = [smalls_ref[0, g].astype(f32) for g in range(8)]
@@ -586,7 +598,7 @@
     def project(slot):
         here = slice(slot * group, (slot + 1) * group)
         for c in range(3):
-            proj_ref[c, :, here] = dot_nn(normed_ref[...], wqs_ref[c, :, here]).astype(bf16)
+            proj_ref[c, :, here] = dot_nn(normed_ref[...], wqs_ref[slot, :, c].reshape(width, group)).astype(bf16)
 
     def attend(pair):
         attend_front(pair, proj_ref, span_ref, tile_ref, attended_ref, lse_ref, kept_ref)
@@ -600,17 +612,12 @@
     for copy in wo_z:
         copy.wait_recv()
     wo_x = [send(out_part(x, 0, 4), out_part(x, 0, 4), (other, z)) for other in near]
+    attend(0)
     second_on = []
     for j in range(3):
         owner = across[j]
         wq_second[j].wait_recv()
         second_on.append(send(qkv_part(owner, 1), qkv_part(owner, 1), (sibling, z)))
-    attend(0)
-    wo_on = []
-    for j in range(3):
-        owner = across[j]
-        wo_x[j].wait_recv()
-        wo_on.append(send(out_part(owner, 0, 4), out_part(owner, 0, 4), (sibling, z)))
     attend(1)
     got_0 = exchange(0)
     for copy in [wq_second[3]] + second_on:
@@ -625,8 +632,15 @@
     attend(2)
     attend(3)
     got_1 = exchange(1)
+    wo_on = []
+    for j in range(3):
+        owner = across[j]
+        wo_x[j].wait_recv()
+        wo_on.append(send(out_part(owner, 0, 4), out_part(owner, 0, 4), (sibling, z)))
     for copy in [wo_x[3]] + wo_on:
         copy.wait_recv()
+    for owner in range(8):
+        wos_ref[:, owner * depth:(owner + 1) * depth] = wos_in_ref[owner]
     outs.append(pltpu.make_async_copy(wos_ref, wos_out, out_sem.at[3]))
     outs[3].start()
     own = pl.ds(pl.multiple_of(half * rows, rows), rows)
@@ -634,6 +648,48 @@
     for copy in (got_0, got_1):
         copy.wait_recv()
     att_ref[:, 2 * group:] = got_ref[...]
+
+    gain_second = jnp.concatenate([part[17:18, :] for part in own_smalls], axis=1)
+    experts = rows_ref.shape[0]
+    router = jnp.concatenate([part[:experts, :] for part in own_smalls], axis=1)
+    router = jnp.concatenate([router, jnp.zeros((depth - experts, width), f32)], axis=0).astype(bf16)
+    lanes_f = lanes.astype(f32)
+    for i in range(2):
+        here = slice(i * step, (i + 1) * step)
+        hidden = seq_ref[half, here, :].astype(f32) + dot_nn(att_ref[here, :], wos_ref[...])
+        hidden_ref[here, :] = hidden
+        normed, _ = normalize(hidden)
+        second = (normed * gain_second).astype(bf16)
+        second_ref[here, :] = second
+        logits = jnp.where(lanes < experts, dot_nt(second, router), -1e30)
+        route = jnp.exp(logits - jnp.max(logits, axis=1, keepdims=True))
+        route = route / jnp.sum(route, axis=1, keepdims=True)
+        ids = ids_ref[here, :]
+        gates = []
+        for c in range(2):
+            gate = jnp.sum(jnp.where(lanes_f == ids[:, experts + 4 + c:experts + 5 + c], route, 0.0), axis=1, keepdims=True)
+            gates.append(jnp.where(ids[:, experts + 2 + c:experts + 3 + c] >= 0.0, gate, 0.0))
+            high = gates[c].astype(bf16).astype(f32)
+            gate_parts_ref[c, here, :] = jnp.where(
+                lanes == 0, high, jnp.where(lanes == 1, gates[c] - high, 0.0)
+            ).astype(bf16)
+        cols_ref[here, :] = jnp.where(
+            lanes < experts, route, jnp.where(lanes == experts, gates[0], jnp.where(lanes == experts + 1, gates[1], ids))
+        )
+    for i in range(4):
+        first, second = marks(i)
+        rows_ref[i * blocks:(i + 1) * blocks] = (
+            dot_nn(first + second, second_ref[...]).astype(bf16).reshape(blocks, slots, width)
+        )
+        parts = dot_nn(first, gate_parts_ref[0]) + dot_nn(second, gate_parts_ref[1])
+        for n in range(blocks):
+            turned = parts[n * slots:(n + 1) * slots, :].T
+            line = jnp.concatenate([turned[0:1, :] + turned[1:2, :], jnp.zeros((1, depth - slots), f32)], axis=1)
+            gates_ref[i * blocks + n] = jnp.broadcast_to(line, (8, depth))
+    outs.append(pltpu.make_async_copy(rows_ref, rows_hbm, out_sem.at[4]))
+    outs.append(pltpu.make_async_copy(grads_ref, grads_hbm, out_sem.at[5]))
+    for copy in outs[4:]:
+        copy.start()
     for copy in inner_copies + far_copies:
         copy.wait_recv()
     for copy in started:
@@ -642,7 +698,7 @@
         copy.wait()
 
 
-def run_front(tokens, w_qkv, w_out, small, w_in, grad_rows, picks):
+def run_front(tokens, w_qkv, w_out, small, w_in, cotangent, picks, ids, spots, experts):
     rows, width = tokens.shape
     group = w_qkv.shape[2]
     f32, bf16 = jnp.float32, jnp.bfloat16
@@ -650,10 +706,10 @@
     anywhere = pl.BlockSpec(memory_space=pl.ANY)
     inside = pl.BlockSpec(memory_space=pltpu.VMEM)
     seq = (2, rows, width)
-    wqs = (3, width, 2 * group)
+    wqs = (2, 8) + w_qkv.shape
     wos = (width, width)
     smalls = (4, 8) + small.shape
-    copies_count = 3 + 1 + 4 + 1 + 3 + 4 + 4 + 3 + 3 + 4 + 3 + 3 + 2 + 2 + 8
+    copies_count = 3 + 1 + 4 + 1 + 3 + 4 + 4 + 3 + 3 + 4 + 3 + 3 + 3 + 2 + 8
     return pl.pallas_call(
         front_kernel,
         out_shape=(
@@ -665,51 +721,54 @@
             jax.ShapeDtypeStruct((rows, width), bf16),
             jax.ShapeDtypeStruct((heads // 2, 2, 2 * rows), f32),
             jax.ShapeDtypeStruct((heads, 2, BLK, BLK), bf16),
+            jax.ShapeDtypeStruct((rows, width), f32),
+            jax.ShapeDtypeStruct((rows, 128), f32),
+            jax.ShapeDtypeStruct((experts, 8, 128), f32),
+            jax.ShapeDtypeStruct((experts, CAP, width), bf16),
+            jax.ShapeDtypeStruct((experts, CAP, width), bf16),
             jax.ShapeDtypeStruct(w_in.shape[1:], bf16),
             jax.ShapeDtypeStruct(w_in.shape[1:], bf16),
-            jax.ShapeDtypeStruct((2, 4) + grad_rows.shape[1:], bf16),
+            jax.ShapeDtypeStruct(w_in.shape[1:], bf16),
+            jax.ShapeDtypeStruct((2, 4, CAP, width), bf16),
         ),
-        in_specs=[anywhere] * 6 + [inside],
-        out_specs=(anywhere,) * 4 + (inside,) * 4 + (anywhere,) * 3,
+        in_specs=[anywhere] * 6 + [inside] * 3,
+        out_specs=(anywhere,) * 4 + (inside,) * 7 + (anywhere,) * 6,
         scratch_shapes=[
             pltpu.VMEM(seq, bf16),
             pltpu.VMEM(wqs, bf16),
             pltpu.VMEM(wos, bf16),
+            pltpu.VMEM((8, width, width // 8), bf16),
             pltpu.VMEM(smalls, bf16),
             pltpu.VMEM((2 * rows, width), bf16),
             pltpu.VMEM((2 * rows, 2 * group), bf16),
             pltpu.VMEM((rows, 2 * group), bf16),
             pltpu.VMEM((2, heads, 2 * BLK), f32),
             pltpu.VMEM((2, 2, BLK, BLK), f32),
+            pltpu.VMEM((rows, width), bf16),
+            pltpu.VMEM((experts, CAP, width), bf16),
+            pltpu.VMEM((experts, CAP, width), bf16),
+            pltpu.VMEM((rows, width), bf16),
+            pltpu.VMEM((2, rows, 128), bf16),
             pltpu.SemaphoreType.DMA((copies_count,)),
             pltpu.SemaphoreType.DMA((copies_count,)),
-            pltpu.SemaphoreType.DMA((4,)),
-            pltpu.SemaphoreType.DMA((4,)),
+            pltpu.SemaphoreType.DMA((5,)),
+            pltpu.SemaphoreType.DMA((6,)),
         ],
         compiler_params=pltpu.CompilerParams(
             collective_id=0, has_side_effects=True, vmem_limit_bytes=56 * 2**20
         ),
         cost_estimate=pl.CostEstimate(flops=60 * 10**9, bytes_accessed=30 * 2**20, transcendentals=0),
         name="run_front",
-    )(tokens, w_qkv, w_out, small, w_in, grad_rows, picks)
-
-
-def swap_z(values, step):
-    return lax.ppermute(values, "gy", [(i, i ^ step) for i in range(4)])
-
-
-def exchange_chips(blocks):
-    groups = [[2 * c + h for c in range(4)] for h in range(2)]
-    return lax.all_to_all(blocks, "gx", 0, 0, axis_index_groups=groups, tiled=True)
+    )(tokens, w_qkv, w_out, small, w_in, cotangent, picks, ids, spots)
 
 
 def expert_kernel(
-    rows_ref, gates_ref, grads_ref, far_ref, inner_ref, inner_a_ref, inner_b_ref, outer_ref,
-    returned_ref, copies_ref, ginner_ref, gouter_ref, inner_in_ref,
+    rows_ref, gates_ref, grads_ref, far_ref, inner_ref, inner_a_ref, inner_b_ref, inner_c_ref, outer_ref,
+    returned_ref, copies_ref, ginner_ref, ginner_sent_ref, gouter_ref, inner_in_ref, outer_land_ref,
     x_ref, x_t_ref, dy_ref, gates_in_ref, win_ref, wout_ref, upper_ref, hid_ref, out_ref, back_ref,
     stage_in_ref, stage_out_ref, add_in_ref, outer_in_ref,
     row_send, row_recv, gate_send, gate_recv, out_send, out_recv, copy_send, copy_recv,
-    grad_send, grad_recv, w_send, w_recv, part_send, part_recv, gout_send, gout_recv, local_sem, join_sem,
+    grad_send, grad_recv, w_send, w_recv, part_send, part_recv, gout_send, gout_recv, local_sem, join_sem, load_sem,
 ):
     x, z, along_z, across, sibling = places()
     core = x % 2
@@ -772,29 +831,31 @@
         pltpu.make_async_copy(inner_a_ref, win_ref.at[chips[1], core], local_sem.at[1]),
         pltpu.make_async_copy(inner_b_ref, win_ref.at[chips[2], core], local_sem.at[2]),
         pltpu.make_async_copy(grads_ref.at[me], dy_ref.at[0, chip], local_sem.at[3]),
+        pltpu.make_async_copy(inner_c_ref, win_ref.at[chips[3], core], local_sem.at[10]),
         pltpu.make_async_copy(rows_ref.at[me], x_ref.at[0, chip], local_sem.at[4]),
         pltpu.make_async_copy(gates_ref.at[me], gates_in_ref.at[0, chip], local_sem.at[5]),
         pltpu.make_async_copy(outer_ref.at[chip], wout_ref.at[:, lanes_of(x)], local_sem.at[6]),
     ]
     pair_inner = [
         remote(source, win_ref.at[chips[k], core], (w_send, w_recv), k, pair)
-        for k, source in enumerate((inner_ref.at[chip], inner_a_ref, inner_b_ref))
-    ]
-    far_inner = remote(inner_ref.at[chips[3]], win_ref.at[chip, core], (w_send, w_recv), 3, (across[2], z))
-    far_block = win_ref.at[chips[3], core]
-    pair_far = remote(far_block, far_block, (w_send, w_recv), 11, pair)
+        for k, source in enumerate((inner_ref.at[chip], inner_a_ref, inner_b_ref, inner_c_ref))
+    ]
     outer_copies = [
-        remote(outer_ref.at[device // 2], wout_ref.at[:, lanes_of(x)], (w_send, w_recv), 4 + j, (device, z))
+        remote(outer_ref.at[device // 2], outer_land_ref.at[x], (w_send, w_recv), 4 + j, (device, z))
         for j, device in enumerate(across)
     ]
-    pair_outer = [remote(outer_ref.at[chip], wout_ref.at[:, lanes_of(x)], (w_send, w_recv), 7, pair)] + [
-        remote(wout_ref.at[:, lanes_of(device)], wout_ref.at[:, lanes_of(device)], (w_send, w_recv), 8 + j, pair)
+    pair_outer = [remote(outer_ref.at[chip], outer_land_ref.at[x], (w_send, w_recv), 7, pair)] + [
+        remote(outer_land_ref.at[device], outer_land_ref.at[device], (w_send, w_recv), 8 + j, pair)
         for j, device in enumerate(across)
+    ]
+    owners = across + (sibling,) + tuple(device + 1 - 2 * core for device in across)
+    outer_loads = [
+        pltpu.make_async_copy(outer_land_ref.at[owner], wout_ref.at[:, lanes_of(owner)], load_sem.at[n])
+        for n, owner in enumerate(owners)
     ]
     for m in ROW_ORDER:
         for copy in row_copies[m]:
             copy.start()
-    far_inner.start()
     for copy in keeps + pair_inner + outer_copies + pair_outer[:1]:
         copy.start()
     for m in range(4):
@@ -812,9 +873,6 @@
         copy.wait()
     for copy in pair_inner:
         copy.wait()
-    far_inner.wait_recv()
-    pair_far.start()
-    pair_far.wait()
 
     def cols(tile, part):
         return pl.ds(pl.multiple_of(part * hidden + tile * half, half), half)
@@ -873,9 +931,13 @@
     for j, copy in enumerate(outer_copies):
         copy.wait_recv()
         pair_outer[1 + j].start()
-    for copy in outer_copies:
+        outer_loads[j].start()
+    for j, copy in enumerate(pair_outer):
+        copy.wait_recv()
+        outer_loads[3 + j].start()
+    for copy in outer_copies + pair_outer:
         copy.wait_send()
-    for copy in pair_outer:
+    for copy in outer_loads:
         copy.wait()
     for m in range(4):
         if m >= 2:
@@ -1045,6 +1107,16 @@
     for tile in (tiles - 2, tiles - 1):
         for copy in inner_stores(tile):
             copy.wait()
+    sent = ginner_sent_ref.shape[2]
+    sent_copies = [
+        remote(
+            ginner_ref.at[device // 2, :, pl.ds(0, sent)], ginner_sent_ref.at[j], (gout_send, gout_recv), 3 + j,
+            (device, z),
+        )
+        for j, device in enumerate(across)
+    ]
+    for copy in sent_copies:
+        copy.start()
     own_out.wait()
     own_copy.wait()
     own_gout.wait()
@@ -1053,8 +1125,7 @@
             copy.wait_send()
         for copy in out_copies[m] + copy_copies[m]:
             copy.wait()
-    far_inner.wait_send()
-    for copy in gout_copies:
+    for copy in gout_copies + sent_copies:
         copy.wait()
 
 
@@ -1078,10 +1149,11 @@
         pltpu.SemaphoreType.DMA((12,)),
         pltpu.SemaphoreType.DMA((2 * tiles,)),
         pltpu.SemaphoreType.DMA((2 * tiles,)),
-        pltpu.SemaphoreType.DMA((3,)),
-        pltpu.SemaphoreType.DMA((3,)),
-        pltpu.SemaphoreType.DMA((10,)),
         pltpu.SemaphoreType.DMA((6,)),
+        pltpu.SemaphoreType.DMA((6,)),
+        pltpu.SemaphoreType.DMA((11,)),
+        pltpu.SemaphoreType.DMA((6,)),
+        pltpu.SemaphoreType.DMA((7,)),
     ]
     outs = pl.pallas_call(
         expert_kernel,
@@ -1089,11 +1161,13 @@
             jax.ShapeDtypeStruct(rows.shape, bf16),
             jax.ShapeDtypeStruct(rows.shape, bf16),
             jax.ShapeDtypeStruct(inner.shape, bf16),
+            jax.ShapeDtypeStruct((3, shard, inner.shape[2] // 4), bf16),
             jax.ShapeDtypeStruct((4, tiles, half, shard), bf16),
             jax.ShapeDtypeStruct((tiles, 2, 4, shard, half), bf16),
+            jax.ShapeDtypeStruct((8, hidden, shard), bf16),
         ),
-        in_specs=[anywhere] * 8,
-        out_specs=(anywhere,) * 5,
+        in_specs=[anywhere] * 9,
+        out_specs=(anywhere,) * 7,
         scratch_shapes=[
             pltpu.VMEM((4, 4, slots, width), bf16),
             pltpu.VMEM((4, 2, shard, tokens), bf16),
@@ -1118,7 +1192,7 @@
         ),
         name="run_experts",
     )(rows, gates, grads, far, inner, *inner_others, outer)
-    return outs[0], outs[1], outs[2], outs[3].reshape(outer.shape)
+    return outs[0], outs[1], outs[2], outs[3], outs[4].reshape(outer.shape)
 
 
 def attend_back(pair, proj_ref, dout_ref, lse_ref, tile_ref, dproj_ref, span_ref, dk_ref, dv_ref, near_ref):
@@ -1200,23 +1274,65 @@
             span_ref[2 * pair + h, d:d + 1, :] = along
 
 
-def combine_kernel(
+def back_kernel(
     returned_hbm, copies_hbm, hidden_hbm, cot_hbm, cols_hbm, wo_hbm, att_hbm, router_ref, gains_ref, counts_ref,
-    mixed_ref, ghidden_ref, own_ref, other_ref, gout_ref, sums_ref,
-    returned_ref, copies_ref, hidden_ref, cot_ref, cols_ref, wo_ref, att_ref, gp_ref, load_sem,
+    picks_ref, proj_hbm, lse_hbm, tile_hbm, wq_hbm, seq_hbm, ginner_hbm,
+    mixed_ref, gtok_ref, gqkv_ref, gwo_ref, sums_ref, inner_in_hbm,
+    returned_ref, copies_ref, hidden_ref, cot_ref, cols_ref, wo_ref, att_ref, gp_ref, dout_send_ref,
+    proj_ref, lse_ref, tile_ref, wq_ref, seq_ref, dout_ref, dproj_ref, span_ref, dk_ref, dv_ref,
+    near_ref, turned_ref, first_send_ref, first_in_ref,
+    q_stage_ref, q_in_ref, q_own_ref, q_across_ref, q_z_ref, q_z_in_ref,
+    gout_ref, o_in_ref, o_sum_ref, o_across_ref, o_z_ref, o_z_in_ref,
+    s_own_ref, s_in_ref, s_sum_ref, s_across_ref, s_z_ref, s_z_in_ref,
+    send_sem, recv_sem, load_sem,
 ):
+    x, z, along_z, across, sibling = places()
+    core = x % 2
+    chip = x // 2
+    half = z % 2
     f32, bf16 = jnp.float32, jnp.bfloat16
-    rows, width = ghidden_ref.shape
+    rows, width = gtok_ref.shape
     shard = width // 8
+    step = rows // 2
+    group = gqkv_ref.shape[2]
     experts = returned_ref.shape[0] // CAP
+    pair = (sibling, z)
+    chips = [(device, z) for device in across]
+    lines = [(x, other) for other in along_z]
+    barrier = pltpu.get_barrier_semaphore()
+    for peer in chips + lines + [pair]:
+        pl.semaphore_signal(barrier, inc=1, device_id=peer, device_id_type=MESH_ID)
     loads = {}
     for name, source, target in (
         ("cols", cols_hbm, cols_ref), ("returned", returned_hbm, returned_ref), ("hidden", hidden_hbm, hidden_ref),
         ("cot", cot_hbm, cot_ref), ("copies", copies_hbm, copies_ref), ("wo", wo_hbm, wo_ref),
-        ("att", att_hbm, att_ref),
+        ("att", att_hbm, att_ref), ("seq", seq_hbm, seq_ref), ("proj", proj_hbm, proj_ref),
+        ("lse", lse_hbm, lse_ref), ("tile", tile_hbm, tile_ref), ("wq", wq_hbm, wq_ref),
     ):
         loads[name] = pltpu.make_async_copy(source, target, load_sem.at[len(loads)])
         loads[name].start()
+    pl.semaphore_wait(barrier, 7)
+    started = []
+
+    def send(source, target, device):
+        index = len(started)
+        copy = pltpu.make_async_remote_copy(
+            src_ref=source, dst_ref=target, send_sem=send_sem.at[index], recv_sem=recv_sem.at[index],
+            device_id=device, device_id_type=MESH_ID,
+        )
+        copy.start()
+        started.append(copy)
+        return copy
+
+    inner_rest = inner_in_hbm.shape[2]
+    inner_copies = [
+        send(
+            ginner_hbm.at[device // 2, :, pl.ds(ginner_hbm.shape[2] - inner_rest, inner_rest)], inner_in_hbm.at[j],
+            (device, z),
+        )
+        for j, device in enumerate(across)
+    ]
+
     gain_second = gains_ref[1:2, :]
     router_t = router_ref[...]
     step = rows // 2
@@ -1259,108 +1375,22 @@
         grad_hidden = grad_mixed + scale * (
             grad_normed - normed * jnp.mean(grad_normed * normed, axis=-1, keepdims=True)
         )
-        ghidden_ref[here, :] = grad_hidden
+        hidden_ref[here, :] = grad_hidden
         gp_ref[here, :] = grad_hidden.astype(bf16)
 
 
     loads["wo"].wait()
-    own_width = own_ref.shape[1]
-    other_ref[...] = dot_nt(gp_ref[...], wo_ref[own_width:, :]).astype(bf16)
-    own_ref[...] = dot_nt(gp_ref[...], wo_ref[:own_width, :]).astype(bf16)
+    own_width = dout_ref.shape[1]
+    dout_send_ref[...] = dot_nt(gp_ref[...], wo_ref[own_width:, :]).astype(bf16)
+    own_rows = pl.ds(pl.multiple_of(half * rows, rows), rows)
+    dout_copy = send(dout_send_ref, dout_ref.at[own_rows, :], lines[0])
+    dout_ref[own_rows, :] = dot_nt(gp_ref[...], wo_ref[:own_width, :]).astype(bf16)
+
     loads["att"].wait()
-    gout_ref[...] = dot_nn(att_ref[...].T, gp_ref[...]).astype(bf16)
+    grad_out = dot_nn(att_ref[...].T, gp_ref[...]).astype(bf16)
     for owner in range(8):
-        here = slice(owner * shard, (owner + 1) * shard)
-        target = sums_ref.at[owner // 2, owner % 2]
-        target[0:1, :] = jnp.zeros((1, shard), f32)
-        target[1:2, :] = gain2_sum[:, here]
-        target[2:2 + experts, :] = grad_router[:experts, here]
-        target[18:22, :] = jnp.zeros((4, shard), f32)
-        target[22:23, :] = route_sum
-        target[23:24, :] = jnp.zeros((1, shard), f32)
-
-
-def combine(returned, copies, hidden, cot, cols, wo, att, router_t, gains, counts):
-    rows, width = hidden.shape
-    shard = width // 8
-    f32, bf16 = jnp.float32, jnp.bfloat16
-    anywhere = pl.BlockSpec(memory_space=pl.ANY)
-    inside = pl.BlockSpec(memory_space=pltpu.VMEM)
-    held = (returned, copies, hidden, cot, cols, wo, att)
-    return pl.pallas_call(
-        combine_kernel,
-        out_shape=(
-            jax.ShapeDtypeStruct((rows, width), bf16),
-            jax.ShapeDtypeStruct((rows, width), f32),
-            jax.ShapeDtypeStruct((rows, width // 2), bf16),
-            jax.ShapeDtypeStruct((rows, width // 2), bf16),
-            jax.ShapeDtypeStruct((width, width), bf16),
-            jax.ShapeDtypeStruct((4, 2, 24, shard), f32),
-        ),
-        in_specs=[anywhere] * 7 + [inside] * 3,
-        out_specs=(inside,) * 6,
-        scratch_shapes=[pltpu.VMEM(array.shape, array.dtype) for array in held]
-        + [pltpu.VMEM((rows, width), bf16), pltpu.SemaphoreType.DMA((7,))],
-        compiler_params=pltpu.CompilerParams(vmem_limit_bytes=48 * 2**20),
-        cost_estimate=pl.CostEstimate(flops=8 * 10**9, bytes_accessed=20 * 2**20, transcendentals=0),
-        name="combine",
-    )(*held, router_t, gains, counts)
-
-
-def back_kernel(
-    own_hbm, other_hbm, gout_hbm, sums_hbm, ghidden_hbm, gains_ref, picks_ref, proj_hbm, lse_hbm, tile_hbm, wq_hbm,
-    seq_hbm,
-    gtok_ref, gqkv_ref, gwo_ref, sums_ref,
-    ghidden_ref, proj_ref, lse_ref, tile_ref, wq_ref, seq_ref, dout_ref, dproj_ref, span_ref, dk_ref, dv_ref,
-    near_ref, turned_ref, first_send_ref, first_in_ref,
-    q_stage_ref, q_in_ref, q_own_ref, q_across_ref, q_z_ref, q_z_in_ref,
-    gout_ref, o_in_ref, o_sum_ref, o_across_ref, o_z_ref, o_z_in_ref,
-    s_own_ref, s_in_ref, s_sum_ref, s_across_ref, s_z_ref, s_z_in_ref,
-    send_sem, recv_sem, load_sem,
-):
-    x, z, along_z, across, sibling = places()
-    core = x % 2
-    chip = x // 2
-    half = z % 2
-    f32, bf16 = jnp.float32, jnp.bfloat16
-    rows, width = gtok_ref.shape
-    shard = width // 8
-    step = rows // 2
-    group = gqkv_ref.shape[2]
-    pair = (sibling, z)
-    chips = [(device, z) for device in across]
-    lines = [(x, other) for other in along_z]
-    barrier = pltpu.get_barrier_semaphore()
-    for peer in chips + lines + [pair]:
-        pl.semaphore_signal(barrier, inc=1, device_id=peer, device_id_type=MESH_ID)
-    loads = {}
-    for name, source, target in (
-        ("gout", gout_hbm, gout_ref), ("proj", proj_hbm, proj_ref),
-        ("own", own_hbm, dout_ref.at[pl.ds(pl.multiple_of(half * rows, rows), rows), :]),
-        ("other", other_hbm, dout_ref.at[pl.ds(pl.multiple_of((1 - half) * rows, rows), rows), :]),
-        ("lse", lse_hbm, lse_ref), ("tile", tile_hbm, tile_ref), ("seq", seq_hbm, seq_ref), ("wq", wq_hbm, wq_ref),
-        ("sums", sums_hbm, s_own_ref), ("ghidden", ghidden_hbm, ghidden_ref),
-    ):
-        loads[name] = pltpu.make_async_copy(source, target, load_sem.at[len(loads)])
-        loads[name].start()
-    pl.semaphore_wait(barrier, 7)
-    started = []
-
-    def send(source, target, device):
-        index = len(started)
-        copy = pltpu.make_async_remote_copy(
-            src_ref=source, dst_ref=target, send_sem=send_sem.at[index], recv_sem=recv_sem.at[index],
-            device_id=device, device_id_type=MESH_ID,
-        )
-        copy.start()
-        started.append(copy)
-        return copy
-
-    def lanes_of(owner):
-        return pl.ds(pl.multiple_of(owner * shard, shard), shard)
-
-    loads["gout"].wait()
-    o_pair = [send(gout_ref.at[:, lanes_of(2 * j + 1 - core)], o_in_ref.at[j], pair) for j in range(4)]
+        gout_ref[owner // 2, owner % 2] = grad_out[:, owner * shard:(owner + 1) * shard]
+    o_pair = [send(gout_ref.at[j, 1 - core], o_in_ref.at[j], pair) for j in range(4)]
 
     gain_first = gains_ref[0:1, :]
     loads["seq"].wait()
@@ -1370,8 +1400,9 @@
             (normed * gain_first).astype(bf16).T.reshape(4, 2, shard, step)
         )
 
-    for name in ("proj", "lse", "tile", "own", "other"):
+    for name in ("proj", "lse", "tile"):
         loads[name].wait()
+    dout_copy.wait_recv()
 
     def attend(number):
         attend_back(
@@ -1413,7 +1444,7 @@
     for copy in o_pair:
         copy.wait_recv()
     for j in range(4):
-        o_sum_ref[j] = (gout_ref[:, lanes_of(2 * j + core)].astype(f32) + o_in_ref[j].astype(f32)).astype(bf16)
+        o_sum_ref[j] = (gout_ref[j, core].astype(f32) + o_in_ref[j].astype(f32)).astype(bf16)
     o_chips = [send(o_sum_ref.at[device // 2], o_across_ref.at[j], chips[j]) for j, device in enumerate(across)]
     weigh_own(1)
     q_chips_1 = to_chips(1, q_pair_1)
@@ -1425,10 +1456,10 @@
     for turn, side in enumerate((1 - half, half)):
         for i in range(2):
             here = pl.ds(pl.multiple_of(side * rows + i * step, step), step)
-            part = (
-                dot_nt(dproj_ref[0, here, :], wq_ref[0])
-                + dot_nt(dproj_ref[1, here, :], wq_ref[1])
-                + dot_nt(dproj_ref[2, here, :], wq_ref[2])
+            part = sum(
+                dot_nt(dproj_ref[c, here, slot * group:(slot + 1) * group], wq_ref[slot, :, c].reshape(width, group))
+                for slot in range(2)
+                for c in range(3)
             )
             normed, _ = normalize(seq_ref[side, i * step:(i + 1) * step, :].astype(f32))
             gain1_sum = gain1_sum + jnp.sum(part * normed, axis=0, keepdims=True)
@@ -1440,7 +1471,6 @@
             first_copy = send(first_send_ref, first_in_ref, lines[0])
             q_pair_0 = weigh_other(0)
 
-    loads["sums"].wait()
     table = None
     for d in range(2):
         along = span_ref[:, d, :]
@@ -1458,6 +1488,10 @@
         here = slice(owner * shard, (owner + 1) * shard)
         target = s_own_ref.at[owner // 2, owner % 2]
         target[0:1, :] = gain1_sum[:, here]
+        target[1:2, :] = gain2_sum[:, here]
+        target[2:2 + experts, :] = grad_router[:experts, here]
+        target[22:23, :] = route_sum
+        target[23:24, :] = jnp.zeros((1, shard), f32)
         target[18:22, :] = placed[4 * owner:4 * owner + 4, :]
     s_pair = send(s_own_ref.at[:, 1 - core], s_in_ref, pair)
     weigh_own(0)
@@ -1485,12 +1519,11 @@
     gqkv_ref[...] = chip_total(0, q_chips_0)
 
     first_copy.wait_recv()
-    loads["ghidden"].wait()
     for i in range(2):
         here = slice(i * step, (i + 1) * step)
         grad = (gtok_ref[here, :] + first_in_ref[here, :].astype(f32)) * gain_first
         normed, scale = normalize(seq_ref[half, here, :].astype(f32))
-        gtok_ref[here, :] = ghidden_ref[here, :] + scale * (
+        gtok_ref[here, :] = hidden_ref[here, :] + scale * (
             grad - normed * jnp.mean(grad * normed, axis=-1, keepdims=True)
         )
     q_line.wait_recv()
@@ -1500,33 +1533,47 @@
     gwo_ref[...] += o_z_in_ref[0].astype(f32) + o_z_in_ref[1].astype(f32) + o_z_in_ref[2].astype(f32)
     sums = s_z_ref[...] + s_z_in_ref[0] + s_z_in_ref[1] + s_z_in_ref[2]
     sums_ref[...] = sums
+    for copy in inner_copies:
+        copy.wait_recv()
     for copy in started:
         copy.wait_send()
 
 
-def run_back(own, other, gout, sums, ghidden, gains, picks, proj, lse, tiles, wq, seq):
-    rows, width = ghidden.shape
+def run_back(
+    returned, copies, hidden, cot, cols, wo, att, router_t, gains, counts, picks, proj, lse, tiles, wq, seq, ginner, sent
+):
+    rows, width = hidden.shape
     length = 2 * rows
     shard = width // 8
-    group = wq.shape[2] // 2
+    group = wq.shape[4]
     rows_out = width // 4
     heads = tiles.shape[0]
     f32, bf16 = jnp.float32, jnp.bfloat16
     anywhere = pl.BlockSpec(memory_space=pl.ANY)
     inside = pl.BlockSpec(memory_space=pltpu.VMEM)
-    copies_count = 4 + 2 + 3 + 3 + 3 + 1 + 1 + 3 + 1 + 3 + 3
+    copies_count = 3 + 1 + 4 + 2 + 3 + 3 + 3 + 1 + 1 + 3 + 1 + 3 + 3
     return pl.pallas_call(
         back_kernel,
         out_shape=(
+            jax.ShapeDtypeStruct((rows, width), bf16),
             jax.ShapeDtypeStruct((rows, width), f32),
             jax.ShapeDtypeStruct((3, shard, group), f32),
             jax.ShapeDtypeStruct((rows_out, shard), f32),
             jax.ShapeDtypeStruct((24, shard), f32),
+            jax.ShapeDtypeStruct((3, shard, ginner.shape[2] - sent), bf16),
         ),
-        in_specs=[anywhere] * 5 + [inside] * 2 + [anywhere] * 5,
-        out_specs=(inside,) * 4,
+        in_specs=[anywhere] * 7 + [inside] * 4 + [anywhere] * 6,
+        out_specs=(inside,) * 5 + (anywhere,),
         scratch_shapes=[
-            pltpu.VMEM(ghidden.shape, f32),
+            pltpu.VMEM(returned.shape, bf16),
+            pltpu.VMEM(copies.shape, bf16),
+            pltpu.VMEM(hidden.shape, f32),
+            pltpu.VMEM(cot.shape, bf16),
+            pltpu.VMEM(cols.shape, f32),
+            pltpu.VMEM(wo.shape, bf16),
+            pltpu.VMEM(att.shape, bf16),
+            pltpu.VMEM((rows, width), bf16),
+            pltpu.VMEM((rows, 2 * group), bf16),
             pltpu.VMEM(proj.shape, bf16),
             pltpu.VMEM(lse.shape, f32),
             pltpu.VMEM(tiles.shape, bf16),
@@ -1547,7 +1594,7 @@
             pltpu.VMEM((2, 3, 3, shard, group), bf16),
             pltpu.VMEM((3, shard, group), bf16),
             pltpu.VMEM((3, shard, group), bf16),
-            pltpu.VMEM((width, width), bf16),
+            pltpu.VMEM((4, 2, width, shard), bf16),
             pltpu.VMEM((4, width, shard), bf16),
             pltpu.VMEM((4, width, shard), bf16),
             pltpu.VMEM((3, width, shard), bf16),
@@ -1561,42 +1608,58 @@
             pltpu.VMEM((3, 24, shard), f32),
             pltpu.SemaphoreType.DMA((copies_count,)),
             pltpu.SemaphoreType.DMA((copies_count,)),
-            pltpu.SemaphoreType.DMA((10,)),
+            pltpu.SemaphoreType.DMA((12,)),
         ],
         compiler_params=pltpu.CompilerParams(
-            collective_id=2, has_side_effects=True, vmem_limit_bytes=60 * 2**20
+            collective_id=2, has_side_effects=True, vmem_limit_bytes=62 * 2**20
         ),
         cost_estimate=pl.CostEstimate(flops=60 * 10**9, bytes_accessed=60 * 2**20, transcendentals=0),
         name="run_back",
-    )(own, other, gout, sums, ghidden, gains, picks, proj, lse, tiles, wq, seq)
+    )(
+        returned, copies, hidden, cot, cols, wo, att, router_t, gains, counts, picks, proj, lse, tiles, wq, seq, ginner
+    )
 
 
 def final_kernel(
-    ginner_hbm, gtok_hbm, gqkv_hbm, gwo_hbm, sums_ref, counts_ref,
-    inner_hbm, tok_hbm, qkv_hbm, wo_hbm, gain1_ref, gain2_ref, grouter_ref, gbias_ref, load_ref, loss_ref,
-    in_ref, out_ref, in_sem, out_sem, copy_sem,
+    ginner_hbm, sent_hbm, rest_hbm, gouter_hbm, mixed_hbm, gtok_hbm, gqkv_hbm, gwo_hbm, sums_ref, counts_ref,
+    inner_hbm, outer_hbm, mixed_out, tok_hbm, qkv_hbm, wo_hbm, gain1_ref, gain2_ref, grouter_ref, gbias_ref, load_ref,
+    loss_ref,
+    in_ref, out_ref, slim_in_ref, slim_out_ref, mixed_ref, tok_ref, qkv_ref, wo_ref, in_sem, out_sem, copy_sem,
 ):
-    z = lax.axis_index("gy")
+    x, z, _, across, _ = places()
+    chip = x // 2
     f32 = jnp.float32
-    copies = [
-        pltpu.make_async_copy(source, target, copy_sem.at[n])
-        for n, (source, target) in enumerate(((gtok_hbm, tok_hbm), (gqkv_hbm, qkv_hbm), (gwo_hbm, wo_hbm)))
-    ]
+    passed = (
+        (mixed_hbm, mixed_ref, mixed_out), (gtok_hbm, tok_ref, tok_hbm), (gqkv_hbm, qkv_ref, qkv_hbm),
+        (gwo_hbm, wo_ref, wo_hbm),
+    )
+    copies_in = [pltpu.make_async_copy(a, b, copy_sem.at[n]) for n, (a, b, _) in enumerate(passed)]
+    copies = [pltpu.make_async_copy(b, c, copy_sem.at[4 + n]) for n, (_, b, c) in enumerate(passed)]
     depth, _, wide = in_ref.shape
-    blocks = [
-        (n, pl.ds(part * wide, wide)) for n in range(ginner_hbm.shape[0]) for part in range(ginner_hbm.shape[2] // wide)
-    ]
+    slim = slim_in_ref.shape[1]
+    sent = sent_hbm.shape[2]
+    jobs = []
+    for part in range(ginner_hbm.shape[2] // wide):
+        here = pl.ds(part * wide, wide)
+        jobs.append((ginner_hbm.at[chip, :, here], inner_hbm.at[chip, :, here], in_ref, out_ref))
+        for j, device in enumerate(across):
+            source = sent_hbm.at[j, :, here] if part * wide < sent else rest_hbm.at[j, :, pl.ds(part * wide - sent, wide)]
+            jobs.append((source, inner_hbm.at[device // 2, :, here], in_ref, out_ref))
+    for n in range(gouter_hbm.shape[0]):
+        for i in range(gouter_hbm.shape[1] // slim):
+            here = pl.ds(i * slim, slim)
+            jobs.append((gouter_hbm.at[n, here], outer_hbm.at[n, here], slim_in_ref, slim_out_ref))
     loads = [
-        pltpu.make_async_copy(ginner_hbm.at[n, :, here], in_ref.at[i % depth], in_sem.at[i % depth])
-        for i, (n, here) in enumerate(blocks)
+        pltpu.make_async_copy(source, held.at[i % depth], in_sem.at[i % depth])
+        for i, (source, _, held, _) in enumerate(jobs)
     ]
     stores = [
-        pltpu.make_async_copy(out_ref.at[i % depth], inner_hbm.at[n, :, here], out_sem.at[i % depth])
-        for i, (n, here) in enumerate(blocks)
+        pltpu.make_async_copy(held.at[i % depth], target, out_sem.at[i % depth])
+        for i, (_, target, _, held) in enumerate(jobs)
     ]
     for i in range(depth - 1):
         loads[i].start()
-    for copy in copies:
+    for copy in copies_in:
         copy.start()
     experts = load_ref.shape[1]
     heads = gbias_ref.shape[1]
@@ -1612,13 +1675,16 @@
     prob_sums = sums[22:23, :experts]
     load_ref[...] = jnp.concatenate([experts * counts / pairs_in_all, experts * prob_sums / tokens], axis=0)
     loss_ref[...] = experts * jnp.sum(counts / pairs_in_all * (prob_sums / tokens), axis=1, keepdims=True)
-    for i in range(len(blocks)):
-        if i + depth - 1 < len(blocks):
+    for copy_in, copy in zip(copies_in, copies):
+        copy_in.wait()
+        copy.start()
+    for i, (_, _, held_in, held_out) in enumerate(jobs):
+        if i + depth - 1 < len(jobs):
             loads[i + depth - 1].start()
         loads[i].wait()
         if i >= depth:
             stores[i - depth].wait()
-        out_ref[i % depth] = in_ref[i % depth].astype(f32)
+        held_out[i % depth] = held_in[i % depth].astype(f32)
         stores[i].start()
     for store in stores[-depth:]:
         store.wait()
@@ -1626,16 +1692,19 @@
         copy.wait()
 
 
-def finish(ginner, gtok, gqkv, gwo, sums, counts, experts, heads):
+def finish(ginner, sent, rest, gouter, mixed, gtok, gqkv, gwo, sums, counts, experts, heads):
     f32, bf16 = jnp.float32, jnp.bfloat16
     local, shard, inner_width = ginner.shape
     wide = inner_width // 4
+    slim = gouter.shape[1] // 2
     anywhere = pl.BlockSpec(memory_space=pl.ANY)
     inside = pl.BlockSpec(memory_space=pltpu.VMEM)
     return pl.pallas_call(
         final_kernel,
         out_shape=(
             jax.ShapeDtypeStruct(ginner.shape, f32),
+            jax.ShapeDtypeStruct(gouter.shape, f32),
+            jax.ShapeDtypeStruct(mixed.shape, bf16),
             jax.ShapeDtypeStruct(gtok.shape, f32),
             jax.ShapeDtypeStruct(gqkv.shape, f32),
             jax.ShapeDtypeStruct(gwo.shape, f32),
@@ -1646,19 +1715,25 @@
             jax.ShapeDtypeStruct((2, experts), f32),
             jax.ShapeDtypeStruct((1, 1), f32),
         ),
-        in_specs=[anywhere] * 4 + [inside] * 2,
-        out_specs=(anywhere,) * 4 + (inside,) * 6,
+        in_specs=[anywhere] * 8 + [inside] * 2,
+        out_specs=(anywhere,) * 6 + (inside,) * 6,
         scratch_shapes=[
             pltpu.VMEM((4, shard, wide), bf16),
             pltpu.VMEM((4, shard, wide), f32),
+            pltpu.VMEM((4, slim, shard), bf16),
+            pltpu.VMEM((4, slim, shard), f32),
+            pltpu.VMEM(mixed.shape, bf16),
+            pltpu.VMEM(gtok.shape, f32),
+            pltpu.VMEM(gqkv.shape, f32),
+            pltpu.VMEM(gwo.shape, f32),
             pltpu.SemaphoreType.DMA((4,)),
             pltpu.SemaphoreType.DMA((4,)),
-            pltpu.SemaphoreType.DMA((3,)),
+            pltpu.SemaphoreType.DMA((8,)),
         ],
-        compiler_params=pltpu.CompilerParams(vmem_limit_bytes=32 * 2**20),
-        cost_estimate=pl.CostEstimate(flops=0, bytes_accessed=24 * 2**20, transcendentals=0),
+        compiler_params=pltpu.CompilerParams(vmem_limit_bytes=62 * 2**20),
+        cost_estimate=pl.CostEstimate(flops=0, bytes_accessed=32 * 2**20, transcendentals=0),
         name="finish",
-    )(ginner, gtok, gqkv, gwo, sums, counts)
+    )(ginner, sent, rest, gouter, mixed, gtok, gqkv, gwo, sums, counts)
 
 
 def fast_device(
@@ -1702,18 +1777,17 @@
         jnp.where(keep, ((expert_ids[:, c] % 4) * 4 + expert_ids[:, c] // 4) * CAP + slots[c], -1)
         for c, keep in enumerate(kept)
     ]
-    buffer_rows = jnp.arange(expert_count * CAP, dtype=jnp.int32)
-    marks = [buffer_rows[:, None] == spot[None] for spot in spots]
-    dispatch = (marks[0] | marks[1]).astype(bf16)
-    grad_rows = jnp.dot(dispatch, cotangent, preferred_element_type=f32).astype(bf16)
-    grad_rows = grad_rows.reshape(expert_count, CAP, model_width)
-
+    spots_float = [spot.astype(f32) for spot in spots]
+    ids = jnp.stack(spots_float + [expert_ids[:, c].astype(f32) for c in range(top_count)], axis=1)
+    ids = jnp.pad(ids, ((0, 0), (expert_count + 2, 128 - expert_count - 6)))
+    spot_rows = jnp.pad(jnp.stack(spots_float), ((0, 8 - top_count), (0, 0)))
     buckets = span_buckets()[:, :, None] == jnp.arange(128, dtype=jnp.int32)
     picks = buckets.astype(bf16)
     (
-        seq_tokens, qkv_weight, out_weight, smalls, projected, attended, log_totals, bias_tiles, inner_a, inner_b,
+        seq_tokens, qkv_weight, out_weight, smalls, projected, attended, log_totals, bias_tiles, hidden_state, columns,
+        gate_rows, send_rows, grad_rows, inner_a, inner_b, inner_c,
         grads_far,
-    ) = run_front(tokens, w_qkv, w_out, small, w_in, grad_rows, picks)
+    ) = run_front(tokens, w_qkv, w_out, small, w_in, cotangent, picks, ids, spot_rows, expert_count)
 
     own_small = smalls[0]
     router_t = own_small[:, :16].transpose(1, 0, 2).reshape(expert_count, model_width)
@@ -1722,68 +1796,52 @@
     all_counts = smalls[:, :, 22:24, :expert_count].astype(f32).sum(axis=(0, 1))
     counts = 32.0 * all_counts[0] + all_counts[1]
 
-    hidden_state = tokens.astype(f32) + jnp.dot(attended, out_weight, preferred_element_type=f32)
-    normed_two, _ = normalize(hidden_state)
-    second_norm = (normed_two * gain_second).astype(bf16)
-    logits = lax.dot_general(second_norm, router_t, (((1,), (1,)), ((), ())), preferred_element_type=f32)
-    route = jax.nn.softmax(logits, axis=-1)
-
-    gates = [
-        jnp.where(keep, jnp.sum(jnp.where(hit, route, 0.0), axis=1), 0.0) for hit, keep in zip(hits, kept)
-    ]
-    gate_rows = jnp.sum(
-        jnp.where(marks[0], gates[0][None], 0.0) + jnp.where(marks[1], gates[1][None], 0.0), axis=1
-    )
-    send_rows = jnp.dot(dispatch, second_norm, preferred_element_type=f32).astype(bf16)
-    gate_rows = jnp.pad(gate_rows.reshape(expert_count, 1, CAP), ((0, 0), (0, 7), (0, 128 - CAP)))
-    returned, grad_copies, grad_inner, grad_outer = run_experts(
-        send_rows.reshape(expert_count, CAP, model_width),
+    returned, grad_copies, grad_inner, grad_sent, grad_outer = run_experts(
+        send_rows,
         gate_rows,
         grad_rows,
         grads_far,
         w_in,
-        (inner_a, inner_b),
+        (inner_a, inner_b, inner_c),
         w_down,
     )
-    grad_inner = exchange_chips(grad_inner)
-    columns = jnp.concatenate(
-        [route] + [column.astype(f32)[:, None] for column in gates + spots + [expert_ids[:, 0], expert_ids[:, 1]]],
-        axis=1,
-    )
-    gains = jnp.stack([gain_first, gain_second])
     count_row = jnp.pad(counts, (0, 128 - expert_count))[None]
-    mixed, grad_hidden, grad_own, grad_other, grad_out_weight, sums = combine(
+    mixed, grad_tokens, grad_qkv, grad_out_weight, sums, grad_rest = run_back(
         returned.reshape(-1, model_width),
         grad_copies.reshape(-1, model_width),
         hidden_state,
         cotangent,
-        jnp.pad(columns, ((0, 0), (0, 128 - columns.shape[1]))),
+        columns,
         out_weight,
         attended,
         jnp.pad(router_t, ((0, 128 - expert_count), (0, 0))),
-        gains,
+        jnp.stack([gain_first, gain_second]),
         count_row,
-    )
-    grad_other, grad_outer = lax.optimization_barrier((swap_z(grad_other, 1), grad_outer.astype(f32)))
-    grad_tokens, grad_qkv, grad_out_weight, sums = run_back(
-        grad_own,
-        grad_other,
-        grad_out_weight,
-        sums,
-        grad_hidden,
-        gains,
         picks,
         projected,
         log_totals,
         bias_tiles,
         qkv_weight,
         seq_tokens,
+        grad_inner,
+        grad_sent.shape[2],
     )
     (
-        grad_inner, grad_tokens, grad_qkv, grad_out_weight, gain_one, gain_two, grad_router, grad_rel_bias, router_load,
-        loss,
+        grad_inner, grad_outer, mixed, grad_tokens, grad_qkv, grad_out_weight, gain_one, gain_two, grad_router,
+        grad_rel_bias, router_load, loss,
     ) = finish(
-        grad_inner, grad_tokens, grad_qkv, grad_out_weight, sums, count_row, expert_count, group_heads
+        grad_inner,
+        grad_sent,
+        grad_rest,
+        grad_outer,
+        mixed,
+        grad_tokens,
+        grad_qkv,
+        grad_out_weight,
+        sums,
+        count_row,
+        expert_count,
+        group_heads,
     )
     return (
         mixed,

time: 514 us -> 474 us (0.922)
  starting transfers between devices: 19.6 us -> 0 us
  matrix products: 11.5 us -> 0.26 us
  waiting for transfers between devices: 8.78 us -> 0 us
    pallas_call x1, Pallas kernels: 239 us -> 209 us  [run_experts(): pl.pallas_call(expert_kernel, out_shape=(jax.ShapeDtypeStruct(rows.shape,...]
    pallas_call x1, Pallas kernels: 75.3 us -> 99.4 us  [run_back(): pl.pallas_call(back_kernel, out_shape=(jax.ShapeDtypeStruct((rows, width)...]
    pallas_call x1, Pallas kernels: 109 us -> 128 us  [run_front(): pl.pallas_call(front_kernel, out_shape=(jax.ShapeDtypeStruct(seq, bf16),...]
    ppermute x1 -> x0, starting transfers between devices: 14.3 us -> none  [swap_z(): return lax.ppermute(values, 'gy', [(i, i ^ step) for i in range(4)])]
    pallas_call x1 -> x0, Pallas kernels: 12.8 us -> none  [combine(): pl.pallas_call(combine_kernel, out_shape=(jax.ShapeDtypeStruct((rows, wid...]
    dot_general x4 -> x0, matrix products: 11.2 us -> none  [the longest x1 4.27 us: fast_device(): jnp.dot(dispatch, cotangent, preferred_element_type=f32).astype(bf16)]
    ppermute x1 -> x0, waiting for transfers between devices: 8.78 us -> none  [swap_z(): return lax.ppermute(values, 'gy', [(i, i ^ step) for i in range(4)])]
    all_to_all x1 -> x0, starting transfers between devices: 5.28 us -> none  [exchange_chips(): lax.all_to_all(blocks, 'gx', 0, 0, axis_index_groups=groups, tiled=True)]
  transfers between devices with their start and end apart: 2 -> 0, of which waited for: 1 -> 0; matrix products, arithmetic and copies ran while one was open for 1% -> 0% of each run, Pallas kernels for 17% -> 0%
where the time goes in v1:
time: 474 us; the launch traced here: 465 us
  Pallas kernels  449 us (95%)
  local copies, waits for them, and re-layouts  9.18 us (2%)
    pallas_call x1, Pallas kernels, run_experts(): pl.pallas_call(expert_kernel, out_shape=(jax.ShapeDtypeStruct(rows.shape,...  209 us
    pallas_call x1, Pallas kernels, run_front(): pl.pallas_call(front_kernel, out_shape=(jax.ShapeDtypeStruct(seq, bf16),...  128 us
    pallas_call x1, Pallas kernels, run_back(): pl.pallas_call(back_kernel, out_shape=(jax.ShapeDtypeStruct((rows, width)...  99.4 us
    pallas_call x1, Pallas kernels, finish(): pl.pallas_call(final_kernel, out_shape=(jax.ShapeDtypeStruct(ginner.shape...  13.4 us

profile of v1, /device:TPU:0, one launch (start us, length us, event | category | flops | bytes accessed | tf_op | source)
XLA Modules:
  0.0 464.7 jit_solution(9630425039822777083)
XLA Ops:
  0.6 0.7 pad.27
  1.3 0.8 fusion.39
  2.1 0.3 select_reduce_fusion.1
  2.4 3.1 concatenate.3.small_ref
  5.6 0.9 fusion.1.picks_ref
  6.5 0.8 fusion.24
  7.3 0.1 copy.35
  7.5 0.8 pad.30.ids_ref
  8.3 0.8 fusion.30
  9.1 0.6 select_maximum_fusion.spots_ref
  9.7 127.7 %run_front.1 = (bf16[2,512,1024]{2,1,0:T(8,128)(2,1)}, bf16[2,8,3,128,256]{4,3,2,1,0:T(8,128)(2,1)}, bf16[1024,1024]{1,0:T(8,128)(2,1)}, bf16[4,8,32,128]{3,2,1,...) custom-call(bf16[512,1024]{1,0:T(8,128)(2,1)} %tok_ref.1, ...), custom_call_target="tpu_custom_call" | custom-call | flops 60000002048 | bytes 31457280 | tf_op jit(solution)/shard_map/run_front/pallas_call | solution.py:713
  137.5 208.9 %run_experts.1 = (bf16[16,80,1024]{2,1,0:T(8,128)(2,1)}, bf16[16,80,1024]{2,1,0:T(8,128)(2,1)}, bf16[4,128,5632]{2,1,0:T(8,128)(2,1)}, bf16[3,128,1408]{2,1,0:T(...) custom-call(bf16[16,80,1024]{2,1,0:T(8,128)(2,1)} %get-tuple-element, ...), custom_call_target="tpu_custom_call" | custom-call | flops 179999997952 | bytes 62914560 | tf_op jit(solution)/shard_map/run_experts/pallas_call | solution.py:1158
  346.3 0.8 slice_bitcast_fusion
  347.2 0.7 pad.32.router_ref
  347.9 0.6 maximum_convert_fusion.gains_ref
  348.5 0.9 convert_reduce_fusion
  349.4 0.5 pad_bitcast_fusion.counts_ref
  349.9 99.4 %run_back.1 = (bf16[512,1024]{1,0:T(8,128)(2,1)}, f32[512,1024]{1,0:T(8,128)}, f32[3,128,256]{2,1,0:T(8,128)}, f32[256,128]{1,0:T(8,128)}, f32[24,128]{1,0:T(8,128)}, /*index=5*/bf16[3,128,4224]{2,1,0:T(8,128)(2,1)}) custom-call(bf16[1280,1024]{1,0:T(8,128)(2,1)} %bitcast.84, bf16[1280,1024]{1,0:T(8,128)(2,1)} %bitcast.85, ...), custom_call_target="tpu_custom_call" | custom-call | flops 60000002048 | bytes 62914560 | tf_op jit(solution)/shard_map/run_back/pallas_call | solution.py:1555
  449.4 13.4 %finish.1 = (f32[4,128,5632]{2,1,0:T(8,128)}, f32[4,2816,128]{2,1,0:T(8,128)}, bf16[512,1024]{1,0:T(8,128)(2,1)}, f32[512,1024]{1,0:T(8,128)}, f32[3,128,256]{2,...) custom-call(bf16[4,128,5632]{2,1,0:T(8,128)(2,1)} %get-tuple-element, ...), custom_call_target="tpu_custom_call" | custom-call | bytes 33554432 | tf_op jit(solution)/shard_map/finish/pallas_call | solution.py:1702
  462.8 1.5 copy.37
  (12 shorter events, 0.1 us)

commit v2 on v1

--- a/solution.py
+++ b/solution.py
@@ -476,7 +476,7 @@
 
 def front_kernel(
     tok_ref, wq_ref, wo_ref, small_ref, inner_ref, cot_hbm, picks_ref, ids_ref, spots_ref,
-    seq_out, wqs_out, wos_out, smalls_out, proj_ref, att_ref, lse_ref, kept_ref, hidden_ref, cols_ref, gates_ref, rows_hbm, grads_hbm, inner_a_ref, inner_b_ref, inner_c_ref, far_ref,
+    seq_out, wqs_out, wos_out, router_ref, gains_ref, counts_ref, proj_ref, att_ref, lse_ref, kept_ref, hidden_ref, cols_ref, gates_ref, rows_hbm, grads_hbm, inner_a_ref, inner_b_ref, inner_c_ref, far_ref,
     seq_ref, wqs_ref, wos_ref, wos_in_ref, smalls_ref, normed_ref, attended_ref, got_ref, span_ref, tile_ref, cot_ref, grads_ref, rows_ref, second_ref, gate_parts_ref,
     send_sem, recv_sem, local_sem, out_sem,
 ):
@@ -625,7 +625,7 @@
     project(1)
     outs = [
         pltpu.make_async_copy(source, target, out_sem.at[n])
-        for n, (source, target) in enumerate(((seq_ref, seq_out), (smalls_ref, smalls_out), (wqs_ref, wqs_out)))
+        for n, (source, target) in enumerate(((seq_ref, seq_out), (wqs_ref, wqs_out)))
     ]
     for copy in outs:
         copy.start()
@@ -641,8 +641,8 @@
         copy.wait_recv()
     for owner in range(8):
         wos_ref[:, owner * depth:(owner + 1) * depth] = wos_in_ref[owner]
-    outs.append(pltpu.make_async_copy(wos_ref, wos_out, out_sem.at[3]))
-    outs[3].start()
+    outs.append(pltpu.make_async_copy(wos_ref, wos_out, out_sem.at[2]))
+    outs[2].start()
     own = pl.ds(pl.multiple_of(half * rows, rows), rows)
     att_ref[:, :2 * group] = attended_ref[own, :]
     for copy in (got_0, got_1):
@@ -653,6 +653,10 @@
     experts = rows_ref.shape[0]
     router = jnp.concatenate([part[:experts, :] for part in own_smalls], axis=1)
     router = jnp.concatenate([router, jnp.zeros((depth - experts, width), f32)], axis=0).astype(bf16)
+    router_ref[...] = router
+    gains_ref[...] = jnp.concatenate([gain, gain_second], axis=0)
+    counted = sum(smalls_ref[j, g].astype(f32) for j in range(4) for g in range(8))
+    counts_ref[...] = 32.0 * counted[22:23, :] + counted[23:24, :]
     lanes_f = lanes.astype(f32)
     for i in range(2):
         here = slice(i * step, (i + 1) * step)
@@ -686,9 +690,9 @@
             turned = parts[n * slots:(n + 1) * slots, :].T
             line = jnp.concatenate([turned[0:1, :] + turned[1:2, :], jnp.zeros((1, depth - slots), f32)], axis=1)
             gates_ref[i * blocks + n] = jnp.broadcast_to(line, (8, depth))
-    outs.append(pltpu.make_async_copy(rows_ref, rows_hbm, out_sem.at[4]))
-    outs.append(pltpu.make_async_copy(grads_ref, grads_hbm, out_sem.at[5]))
-    for copy in outs[4:]:
+    outs.append(pltpu.make_async_copy(rows_ref, rows_hbm, out_sem.at[3]))
+    outs.append(pltpu.make_async_copy(grads_ref, grads_hbm, out_sem.at[4]))
+    for copy in outs[3:]:
         copy.start()
     for copy in inner_copies + far_copies:
         copy.wait_recv()
@@ -716,7 +720,9 @@
             jax.ShapeDtypeStruct(seq, bf16),
             jax.ShapeDtypeStruct(wqs, bf16),
             jax.ShapeDtypeStruct(wos, bf16),
-            jax.ShapeDtypeStruct(smalls, bf16),
+            jax.ShapeDtypeStruct((128, width), bf16),
+            jax.ShapeDtypeStruct((2, width), f32),
+            jax.ShapeDtypeStruct((1, 128), f32),
             jax.ShapeDtypeStruct((3, 2 * rows, 2 * group), bf16),
             jax.ShapeDtypeStruct((rows, width), bf16),
             jax.ShapeDtypeStruct((heads // 2, 2, 2 * rows), f32),
@@ -732,7 +738,7 @@
             jax.ShapeDtypeStruct((2, 4, CAP, width), bf16),
         ),
         in_specs=[anywhere] * 6 + [inside] * 3,
-        out_specs=(anywhere,) * 4 + (inside,) * 7 + (anywhere,) * 6,
+        out_specs=(anywhere,) * 3 + (inside,) * 10 + (anywhere,) * 6,
         scratch_shapes=[
             pltpu.VMEM(seq, bf16),
             pltpu.VMEM(wqs, bf16),
@@ -922,6 +928,7 @@
     own_out = pltpu.make_async_copy(out_ref.at[0, chip], returned_ref.at[me], local_sem.at[7])
     widen(0)
     widen(1)
+    widen(2)
     for m in range(4):
         for copy in row_copies[m]:
             copy.wait_send()
@@ -939,8 +946,8 @@
         copy.wait_send()
     for copy in outer_loads:
         copy.wait()
-    for m in range(4):
-        if m >= 2:
+    for m in (2, 3, 1, 0):
+        if m == 3:
             widen(m)
         narrow(m)
         for copy in out_copies[m]:
@@ -1027,7 +1034,7 @@
         for m in range(4)
     ]
     own_copy = pltpu.make_async_copy(back_ref.at[0, chip], copies_ref.at[me], local_sem.at[8])
-    for first in range(0, 4, BACK_COUNT):
+    for first in range(4 - BACK_COUNT, -1, -BACK_COUNT):
         back(first, BACK_COUNT)
         for m in range(first, first + BACK_COUNT):
             for copy in copy_copies[m]:
@@ -1342,6 +1349,8 @@
     push = loss_weight * experts * (counts / pairs_in_all) / tokens
     slot_lane = lax.broadcasted_iota(jnp.int32, (1, returned_ref.shape[0]), 1).astype(f32)
     expert_lane = lax.broadcasted_iota(jnp.int32, (1, shard), 1).astype(f32)
+    own_width = dout_ref.shape[1]
+    dout_copies = []
     gain2_sum = jnp.zeros((1, width), f32)
     route_sum = jnp.zeros((1, shard), f32)
     grad_router = jnp.zeros((shard, width), f32)
@@ -1376,14 +1385,19 @@
             grad_normed - normed * jnp.mean(grad_normed * normed, axis=-1, keepdims=True)
         )
         hidden_ref[here, :] = grad_hidden
-        gp_ref[here, :] = grad_hidden.astype(bf16)
-
-
-    loads["wo"].wait()
-    own_width = dout_ref.shape[1]
-    dout_send_ref[...] = dot_nt(gp_ref[...], wo_ref[own_width:, :]).astype(bf16)
+        grad_part = grad_hidden.astype(bf16)
+        gp_ref[here, :] = grad_part
+        if i == 0:
+            loads["wo"].wait()
+        dout_send_ref[here, :] = dot_nt(grad_part, wo_ref[own_width:, :]).astype(bf16)
+        for slot in (1, 0) if i == 0 else (1,):
+            lanes = pl.ds(slot * group, group)
+            dout_copies.append(
+                send(dout_send_ref.at[here, lanes], dout_ref.at[pl.ds(half * rows + i * step, step), lanes], lines[0])
+            )
+
+
     own_rows = pl.ds(pl.multiple_of(half * rows, rows), rows)
-    dout_copy = send(dout_send_ref, dout_ref.at[own_rows, :], lines[0])
     dout_ref[own_rows, :] = dot_nt(gp_ref[...], wo_ref[:own_width, :]).astype(bf16)
 
     loads["att"].wait()
@@ -1400,9 +1414,17 @@
             (normed * gain_first).astype(bf16).T.reshape(4, 2, shard, step)
         )
 
+    dout_copies.append(
+        send(
+            dout_send_ref.at[pl.ds(step, step), pl.ds(0, group)],
+            dout_ref.at[pl.ds(half * rows + step, step), pl.ds(0, group)],
+            lines[0],
+        )
+    )
     for name in ("proj", "lse", "tile"):
         loads[name].wait()
-    dout_copy.wait_recv()
+    for n in (0, 2):
+        dout_copies[n].wait_recv()
 
     def attend(number):
         attend_back(
@@ -1448,11 +1470,14 @@
     o_chips = [send(o_sum_ref.at[device // 2], o_across_ref.at[j], chips[j]) for j, device in enumerate(across)]
     weigh_own(1)
     q_chips_1 = to_chips(1, q_pair_1)
+    for n in (1, 3):
+        dout_copies[n].wait_recv()
     attend(0)
     attend(1)
 
     loads["wq"].wait()
     gain1_sum = jnp.zeros((1, width), f32)
+    first_copies = []
     for turn, side in enumerate((1 - half, half)):
         for i in range(2):
             here = pl.ds(pl.multiple_of(side * rows + i * step, step), step)
@@ -1467,8 +1492,9 @@
                 gtok_ref[i * step:(i + 1) * step, :] = part
             else:
                 first_send_ref[i * step:(i + 1) * step, :] = part.astype(bf16)
+                block = pl.ds(i * step, step)
+                first_copies.append(send(first_send_ref.at[block], first_in_ref.at[block], lines[0]))
         if not turn:
-            first_copy = send(first_send_ref, first_in_ref, lines[0])
             q_pair_0 = weigh_other(0)
 
     table = None
@@ -1518,8 +1544,8 @@
     s_lines = [send(s_z_ref, s_z_in_ref.at[j], lines[j]) for j in range(3)]
     gqkv_ref[...] = chip_total(0, q_chips_0)
 
-    first_copy.wait_recv()
     for i in range(2):
+        first_copies[i].wait_recv()
         here = slice(i * step, (i + 1) * step)
         grad = (gtok_ref[here, :] + first_in_ref[here, :].astype(f32)) * gain_first
         normed, scale = normalize(seq_ref[half, here, :].astype(f32))
@@ -1551,7 +1577,7 @@
     f32, bf16 = jnp.float32, jnp.bfloat16
     anywhere = pl.BlockSpec(memory_space=pl.ANY)
     inside = pl.BlockSpec(memory_space=pltpu.VMEM)
-    copies_count = 3 + 1 + 4 + 2 + 3 + 3 + 3 + 1 + 1 + 3 + 1 + 3 + 3
+    copies_count = 3 + 4 + 4 + 2 + 3 + 3 + 3 + 2 + 1 + 3 + 1 + 3 + 3
     return pl.pallas_call(
         back_kernel,
         out_shape=(
@@ -1784,17 +1810,10 @@
     buckets = span_buckets()[:, :, None] == jnp.arange(128, dtype=jnp.int32)
     picks = buckets.astype(bf16)
     (
-        seq_tokens, qkv_weight, out_weight, smalls, projected, attended, log_totals, bias_tiles, hidden_state, columns,
+        seq_tokens, qkv_weight, out_weight, router_t, gains, count_row, projected, attended, log_totals, bias_tiles, hidden_state, columns,
         gate_rows, send_rows, grad_rows, inner_a, inner_b, inner_c,
         grads_far,
     ) = run_front(tokens, w_qkv, w_out, small, w_in, cotangent, picks, ids, spot_rows, expert_count)
-
-    own_small = smalls[0]
-    router_t = own_small[:, :16].transpose(1, 0, 2).reshape(expert_count, model_width)
-    gain_first = own_small[:, 16].reshape(model_width).astype(f32)
-    gain_second = own_small[:, 17].reshape(model_width).astype(f32)
-    all_counts = smalls[:, :, 22:24, :expert_count].astype(f32).sum(axis=(0, 1))
-    counts = 32.0 * all_counts[0] + all_counts[1]
 
     returned, grad_copies, grad_inner, grad_sent, grad_outer = run_experts(
         send_rows,
@@ -1805,7 +1824,6 @@
         (inner_a, inner_b, inner_c),
         w_down,
     )
-    count_row = jnp.pad(counts, (0, 128 - expert_count))[None]
     mixed, grad_tokens, grad_qkv, grad_out_weight, sums, grad_rest = run_back(
         returned.reshape(-1, model_width),
         grad_copies.reshape(-1, model_width),
@@ -1814,8 +1832,8 @@
         columns,
         out_weight,
         attended,
-        jnp.pad(router_t, ((0, 128 - expert_count), (0, 0))),
-        jnp.stack([gain_first, gain_second]),
+        router_t,
+        gains,
         count_row,
         picks,
         projected,

time: 474 us -> 461 us (0.973)
  Pallas kernels: 449 us -> 440 us
    pallas_call x1, Pallas kernels: 99.4 us -> 91.6 us  [run_back(): pl.pallas_call(back_kernel, out_shape=(jax.ShapeDtypeStruct((rows, width)...]
where the time goes in v2:
time: 461 us; the launch traced here: 452 us
  Pallas kernels  440 us (95%)
  local copies, waits for them, and re-layouts  7.1 us (2%)
    pallas_call x1, Pallas kernels, run_experts(): pl.pallas_call(expert_kernel, out_shape=(jax.ShapeDtypeStruct(rows.shape,...  207 us
    pallas_call x1, Pallas kernels, run_front(): pl.pallas_call(front_kernel, out_shape=(jax.ShapeDtypeStruct(seq, bf16),...  128 us
    pallas_call x1, Pallas kernels, run_back(): pl.pallas_call(back_kernel, out_shape=(jax.ShapeDtypeStruct((rows, width)...  91.6 us
    pallas_call x1, Pallas kernels, finish(): pl.pallas_call(final_kernel, out_shape=(jax.ShapeDtypeStruct(ginner.shape...  13.4 us

profile of v2, /device:TPU:0, one launch (start us, length us, event | category | flops | bytes accessed | tf_op | source)
XLA Modules:
  0.0 452.0 jit_solution(17929890627141840767)
XLA Ops:
  0.6 0.7 pad.19
  1.3 0.8 fusion.39
  2.1 0.3 select_reduce_fusion.1
  2.4 3.1 concatenate.3.small_ref
  5.6 0.8 fusion.30
  6.4 0.8 fusion.24
  7.3 0.6 select_maximum_fusion.spots_ref
  7.9 0.1 copy.33
  8.0 0.8 pad.22.ids_ref
  8.9 0.9 fusion.1.picks_ref
  9.8 127.9 %run_front.1 = (bf16[2,512,1024]{2,1,0:T(8,128)(2,1)}, bf16[2,8,3,128,256]{4,3,2,1,0:T(8,128)(2,1)}, bf16[1024,1024]{1,0:T(8,128)(2,1)}, bf16[128,1024]{1,0:T(8,...) custom-call(bf16[512,1024]{1,0:T(8,128)(2,1)} %tok_ref.1, ...), custom_call_target="tpu_custom_call" | custom-call | flops 60000002048 | bytes 31457280 | tf_op jit(solution)/shard_map/run_front/pallas_call | solution.py:717
  137.7 207.3 %run_experts.1 = (bf16[16,80,1024]{2,1,0:T(8,128)(2,1)}, bf16[16,80,1024]{2,1,0:T(8,128)(2,1)}, bf16[4,128,5632]{2,1,0:T(8,128)(2,1)}, bf16[3,128,1408]{2,1,0:T(...) custom-call(bf16[16,80,1024]{2,1,0:T(8,128)(2,1)} %get-tuple-element, ...), custom_call_target="tpu_custom_call" | custom-call | flops 179999997952 | bytes 62914560 | tf_op jit(solution)/shard_map/run_experts/pallas_call | solution.py:1165
  345.0 91.6 %run_back.1 = (bf16[512,1024]{1,0:T(8,128)(2,1)}, f32[512,1024]{1,0:T(8,128)}, f32[3,128,256]{2,1,0:T(8,128)}, f32[256,128]{1,0:T(8,128)}, f32[24,128]{1,0:T(8,128)}, /*index=5*/bf16[3,128,4224]{2,1,0:T(8,128)(2,1)}) custom-call(bf16[1280,1024]{1,0:T(8,128)(2,1)} %bitcast.68, bf16[1280,1024]{1,0:T(8,128)(2,1)} %bitcast.69, ...), custom_call_target="tpu_custom_call" | custom-call | flops 60000002048 | bytes 62914560 | tf_op jit(solution)/shard_map/run_back/pallas_call | solution.py:1581
  436.6 13.4 %finish.1 = (f32[4,128,5632]{2,1,0:T(8,128)}, f32[4,2816,128]{2,1,0:T(8,128)}, bf16[512,1024]{1,0:T(8,128)(2,1)}, f32[512,1024]{1,0:T(8,128)}, f32[3,128,256]{2,...) custom-call(bf16[4,128,5632]{2,1,0:T(8,128)(2,1)} %get-tuple-element, ...), custom_call_target="tpu_custom_call" | custom-call | bytes 33554432 | tf_op jit(solution)/shard_map/finish/pallas_call | solution.py:1728
  450.0 1.5 copy.34
  (9 shorter events, 0.1 us)
